TPU v7x, 128 devices: a whole 4x4x4 slice. The times are simulated.
128 devices in a mesh: seq: 64 (over y_hi, x, z, core), rep: 2 (over y_lo).
Axes of the slice: x: 4, y: 4 (y_hi: 2, y_lo: 2; y = y_hi * 2 + y_lo), z: 4, core: 2. Of those that a mesh axis runs over, the one named last changes fastest.
Arguments:
- tokens: bfloat16 [2, 16384, 768], P('rep', 'seq'), may hold values from -6 to 6
- router: float32 [768], replicated, may hold values from -0.21875 to 0.21875
- gain_one: float32 [768], replicated, may hold values from 0.5 to 1.5
- bias_one: float32 [768], replicated, may hold values from -1.8 to 1.8
- w_query: bfloat16 [768, 768], replicated, may hold values from -0.21875 to 0.21875
- w_key: bfloat16 [768, 768], replicated, may hold values from -0.21875 to 0.21875
- w_value: bfloat16 [768, 768], replicated, may hold values from -0.21875 to 0.21875
- w_out: bfloat16 [768, 768], replicated, may hold values from -0.875 to 0.875
- gain_two: float32 [768], replicated, may hold values from 0.5 to 1.5
- bias_two: float32 [768], replicated, may hold values from -1.8 to 1.8
- w_expand: bfloat16 [768, 3072], replicated, may hold values from -0.21875 to 0.21875
- w_contract: bfloat16 [3072, 768], replicated, may hold values from -0.109375 to 0.109375
- cotangent: bfloat16 [2, 16384, 768], P('rep', 'seq'), may hold values from -6 to 6
- seq_ids: int32 [2, 16384], P('rep', 'seq'), may hold values from 0 to 16384, as said below
- routed_rows: int32 [2, 64, 48], P('rep', 'seq'), may hold values from 0 to 255, as said below
- routed_count: int32 [2, 64], P('rep', 'seq'), may hold values from 16 to 48, as said below
Outputs:
- output: bfloat16 [2, 16384, 768], P('rep', 'seq')
- input_grad: bfloat16 [2, 16384, 768], P('rep', 'seq')
- router_grad: float32 [768], replicated
- gain_one_grad: float32 [768], replicated
- bias_one_grad: float32 [768], replicated
- query_grad: float32 [768, 768], replicated
- key_grad: float32 [768, 768], replicated
- value_grad: float32 [768, 768], replicated
- out_grad: float32 [768, 768], replicated
- gain_two_grad: float32 [768], replicated
- bias_two_grad: float32 [768], replicated
- expand_grad: float32 [768, 3072], replicated
- contract_grad: float32 [3072, 768], replicated
Inputs may be any that keep to these rules, and one draw needn't show every extreme that they name: `seq_ids`: sequence 0 of a group is one document cut into contiguous pieces, piece j at the head of device j, 64 to 128 tokens each, so that its token order is the group's order; every other id names a short document packed whole on one device after that piece; the last token of every device is a document of its own, and on the last device of a group its id is 16384. `routed_rows`: for each device the 48 indices are distinct and include 256 - 1; the first routed_count of them are ascending and name the routed tokens, at least one of them of sequence 0; the others are padding. `routed_count`: some device of every group uses all 48 slots.
All inputs are finite; a program needn't handle non-finite values.
Results may differ from a plain program's by a relative error of at most 0.012.
Values may be sent and summed in bfloat16 or wider, within the bound.
No kernel may reach another device: no remote copies, remote signals or barrier semaphores. Data moves between devices by JAX's collectives and lax.ppermute only.
A program may use at most 256 MiB of HBM per device.

v0:
```python
import functools
import itertools

import jax
import jax.numpy as jnp
import numpy as np
from jax import lax
from jax.experimental import pallas as pl
from jax.experimental.pallas import tpu as pltpu
from jax.sharding import Mesh
from jax.sharding import PartitionSpec as P

HEAD = 64
HEADS = 12
SLOTS = 48
D = 768
FF = 3072
TOK = 256
RUN = 384
EPSILON = 1e-05
NEG_LARGE = -1e30
EXACT = lax.Precision.HIGHEST
SCALE = float(HEAD) ** (-0.5)
F32 = jnp.float32
BF16 = jnp.bfloat16

SIXTEEN = ("yh", "z", "c")
HOLDERS = [yh * 8 + z * 2 + c for c in range(2) for yh in range(2) for z in range(3)]
IDLE = [yh * 8 + 6 + c for yh in range(2) for c in range(2)]
SIZES = {"yh": 2, "x": 4, "z": 4, "c": 2, "yl": 2}


def width_of(axes):
    total = 1
    for axis in axes:
        total *= SIZES[axis]
    return total


def swap(parts, axes):
    return lax.all_to_all(parts, axes, split_axis=0, concat_axis=0, tiled=True)


def spread(part, axes):
    parts = width_of(axes)
    return swap(jnp.broadcast_to(part[None], (parts,) + part.shape), axes)


CHIPS = ("x", "yh", "yl", "z")
SMEM_SPEC = pl.BlockSpec(memory_space=pltpu.SMEM)
ANY_SPEC = pl.BlockSpec(memory_space=pl.ANY)
VMEM_SPEC = pl.BlockSpec(memory_space=pltpu.VMEM)
HBM_SPEC = pl.BlockSpec(memory_space=pltpu.HBM)


CUBE_AXES = ("x", "z", "c")
FIRST = (("x", "z"), ("z", "x"))


def ring_pairs(turn, step):
    pairs = []
    for x in range(4):
        for z in range(4):
            for c in range(2):
                to = {"x": x, "z": z}
                axis = FIRST[c][turn]
                to[axis] = (to[axis] + step) % 4
                pairs.append((x * 8 + z * 2 + c, to["x"] * 8 + to["z"] * 2 + c))
    return pairs


def ring_swap(parts, at, pairs_of, axes):
    mine = [lax.dynamic_index_in_dim(parts, at, 0, keepdims=False)]
    for step in (1, 2, 3):
        part = lax.dynamic_index_in_dim(parts, lax.rem(at + step, 4), 0, keepdims=False)
        mine.append(lax.ppermute(part, axes, pairs_of(step)))
    return mine


EVERY = ("yh", "x", "z", "c", "yl")
UNIT_ORDERS = (("x", "y", "z"), ("z", "x", "y"))


def gather_pairs(orders, stage, step):
    pairs = []
    for place in itertools.product(range(2), range(4), range(4), range(2), range(2)):
        yh, x, z, c, yl = place
        at = {"x": x, "y": yh * 2 + yl, "z": z}
        axis = orders[c][stage]
        at[axis] = (at[axis] + step) % 4
        source = (at["y"] // 2, at["x"], at["z"], c, at["y"] % 2)
        pairs.append(tuple(int(np.ravel_multi_index(p, (2, 4, 4, 2, 2))) for p in (source, place)))
    return pairs


def gather_step(part, orders, stage):
    return [part] + [
        lax.ppermute(part, EVERY, gather_pairs(orders, stage, step)) for step in (1, 2, 3)
    ]


def other_core(pieces):
    return [lax.ppermute(piece, "c", [(0, 1), (1, 0)]) for piece in pieces]


def chip_at(orders, core, me_ref, steps):
    at = {
        axis: (me_ref["xyz".index(axis)] + step) & 3
        for axis, step in zip(orders[core], steps, strict=True)
    }
    return at["x"], at["y"], at["z"]


def steps_to(orders, core, me_ref, chip):
    return [(chip["xyz".index(axis)] - me_ref["xyz".index(axis)]) & 3 for axis in orders[core]]


def dot(left, right, dims, precision=None):
    return lax.dot_general(
        left, right, (dims, ((), ())), precision=precision, preferred_element_type=F32
    )


def mm(left, right):
    return dot(left, right, ((1,), (0,)))


def mm_tn(left, right):
    return dot(left, right, ((0,), (0,)))


def mm_nt(left, right):
    return dot(left, right, ((1,), (1,)))


def layer_norm(values_in, gain_vec, bias_vec):
    center = values_in - jnp.mean(values_in, axis=-1, keepdims=True)
    spread_ = jnp.mean(center * center, axis=-1, keepdims=True)
    inv = lax.rsqrt(spread_ + EPSILON)
    unit = center * inv
    return unit * gain_vec + bias_vec, unit, inv


def layer_norm_back(grad, unit, inv, gain_vec):
    scaled = grad * gain_vec
    mean_one = jnp.mean(scaled, axis=-1, keepdims=True)
    mean_two = jnp.mean(scaled * unit, axis=-1, keepdims=True)
    return inv * (scaled - mean_one - unit * mean_two)


def place_kernel(other, me_ref, *refs):
    units_in, pieces, refs = refs[0], refs[1:5], refs[5:]
    if other:
        refs = refs[6:]
    (
        expand_ref, contract_ref, out_ref, key_ref, value_ref, query_ref, sums_ref, vector_ref,
        land_ref, land_heads_ref, stage_ref, tiles_ref, heads_ref, in_sems, out_sems,
    ) = refs

    def take(i):
        if i < 4:
            rows = pl.ds(i * 16, 16)
            return pltpu.make_async_copy(units_in.at[rows], land_ref.at[rows], in_sems.at[i])
        return pltpu.make_async_copy(pieces[i - 4], land_heads_ref.at[i - 4], in_sems.at[i])

    for i in range(8):
        take(i).start()

    def emit(core):
        for x in range(4):
            take(x).wait()
            for y in range(4):
                for z in range(4):
                    at = x * 16 + y * 4 + z
                    staged = stage_ref.at[x, y * 4 + z]
                    staged[...] = land_ref[at, :, :D].astype(F32)
                    if core == 0:
                        row = (z * 4 + y) * 48
                        cols = pl.ds(x * D, D)
                        target = expand_ref.at[pl.ds(row, 48), cols]
                    else:
                        row = z * D + (x * 4 + y) * 48
                        target = contract_ref.at[pl.ds(row, 48), :]
                    pltpu.make_async_copy(staged, target, out_sems.at[x]).start()

        def unit_shard(unit, at16, cols):
            if core == 0:
                chip = (unit, at16 % 4, at16 // 4)
            else:
                chip = (at16 // 4, at16 % 4, unit)
            x, y, z = chip
            return land_ref[x * 16 + y * 4 + z, :, cols].astype(F32)

        for row in range(8):
            tiles_ref[row * 48 : (row + 1) * 48, :] = jnp.concatenate(
                [
                    unit_shard(unit, row * 2 + half, slice(D, 896))[:, :96]
                    for unit in range(4)
                    for half in range(2)
                ],
                axis=1,
            )
        rows = pl.ds(core * 384, 384)
        copies = [pltpu.make_async_copy(tiles_ref, out_ref.at[rows, :], out_sems.at[4])]
        copies[0].start()
        for at16 in range(16):
            vector_ref[at16] = sum(unit_shard(unit, at16, slice(D, 896)) for unit in range(4))
        for i in range(4, 8):
            take(i).wait()
        for x in range(4):
            for z in range(4):
                for yl in range(2):
                    halves = [
                        land_heads_ref[(x - me_ref[0]) & 3, (yh * 2 + yl) * 4 + z].astype(F32)
                        for yh in range(2)
                    ]
                    at = slice(((x * 4 + z) * 2 + yl) * 24, ((x * 4 + z) * 2 + yl + 1) * 24)
                    for kind in range(3):
                        cols = slice(kind * 192, (kind + 1) * 192)
                        heads_ref[kind, at, :] = jnp.concatenate(
                            [half[:, cols] for half in halves], axis=1
                        )
                    sums_ref[at, :] = halves[0][:, 576:] + halves[1][:, 576:]
        cols = pl.ds(core * 384, 384)
        for kind, target in enumerate((key_ref, value_ref, query_ref)):
            copies.append(
                pltpu.make_async_copy(
                    heads_ref.at[kind], target.at[:, cols], out_sems.at[5 + kind]
                )
            )
            copies[-1].start()
        for k3 in range(4):
            held = stage_ref.at[k3]
            pltpu.make_async_copy(held, held, out_sems.at[k3]).wait()
        for copy in copies:
            copy.wait()

    for core in range(2):
        pl.when((me_ref[3] + other & 1) == core)(functools.partial(emit, core))


def place(me, pieces, before=None):
    before = () if before is None else tuple(before[:6])
    return pl.pallas_call(
        functools.partial(place_kernel, 1 if before else 0),
        out_shape=(
            jax.ShapeDtypeStruct((D, FF), F32),
            jax.ShapeDtypeStruct((FF, D), F32),
        )
        + (jax.ShapeDtypeStruct((D, D), F32),) * 4
        + (jax.ShapeDtypeStruct((D, HEAD), F32), jax.ShapeDtypeStruct((16, 48, 128), F32)),
        in_specs=[SMEM_SPEC]
        + [ANY_SPEC] * 5
        + [ANY_SPEC] * len(before),
        out_specs=(ANY_SPEC,) * 6 + (VMEM_SPEC,) * 2,
        scratch_shapes=[
            pltpu.VMEM((64, 48, 896), BF16),
            pltpu.VMEM((4, 16, 24, 640), BF16),
            pltpu.VMEM((4, 16, 48, D), F32),
            pltpu.VMEM((384, D), F32),
            pltpu.VMEM((3, D, 384), F32),
            pltpu.SemaphoreType.DMA((8,)),
            pltpu.SemaphoreType.DMA((8,)),
        ],
        input_output_aliases={6 + i: i for i in range(6)} if before else {},
        compiler_params=pltpu.CompilerParams(vmem_limit_bytes=40 * 2**20),
        cost_estimate=pl.CostEstimate(flops=0, bytes_accessed=20 * 2**20, transcendentals=0),
    )(me, *pieces, *before)


def embed_kernel(
    count_ref, rows_ref, ids_ref, tokens_ref, gain_ref, bias_ref, wk_hbm, wv_hbm, wq_hbm,
    chunk_ref, normed_ref, routed_ref, w_ref, sems,
):
    for i, w in enumerate((wk_hbm, wv_hbm, wq_hbm)):
        pltpu.make_async_copy(w, w_ref.at[i], sems.at[i]).start()
    places = lax.broadcasted_iota(jnp.int32, (TOK, SLOTS), 0)
    picks = (rows_ref[...] == places).astype(F32).astype(BF16)
    routed = mm_tn(picks, tokens_ref[...])
    gain = gain_ref[...].reshape(1, D)
    bias = bias_ref[...].reshape(1, D)
    normed = layer_norm(routed, gain, bias)[0].astype(BF16)
    routed_ref[...] = routed
    normed_ref[...] = normed
    ids = ids_ref[...]
    halves = jnp.concatenate([ids >> 8, ids & 255] + [jnp.zeros((6, TOK), jnp.int32)], axis=0)
    halves = halves.astype(F32).astype(BF16)
    ids_rows = mm(halves, picks)
    ids_cols = dot(picks, halves, ((0,), (1,)))
    ids_row = ids_rows[0:1] * 256.0 + ids_rows[1:2]
    ids_col = ids_cols[:, 0:1] * 256.0 + ids_cols[:, 1:2]
    slot_row = lax.broadcasted_iota(jnp.int32, (SLOTS, SLOTS), 1)
    slot_col = lax.broadcasted_iota(jnp.int32, (SLOTS, SLOTS), 0)
    count = count_ref[0]
    same = (ids_row == ids_col) & (slot_row < count) & (slot_col < count) | (slot_row == slot_col)
    first = jnp.min(
        jnp.where(same, slot_row.astype(F32), float(SLOTS)), axis=1, keepdims=True
    )
    lanes = lax.broadcasted_iota(jnp.int32, (SLOTS, HEAD), 1)
    slots = lax.broadcasted_iota(jnp.int32, (SLOTS, HEAD), 0)
    is_long = (ids_col == 0.0) & (slots < count)
    marks = jnp.where(lanes == 0, first + 1.0, jnp.where(lanes == 1, count_ref[1] + 1.0, 0.0))
    marks = jnp.where(is_long, 0.0, marks).astype(BF16)
    parts = []
    for i in range(3):
        pltpu.make_async_copy((wk_hbm, wv_hbm, wq_hbm)[i], w_ref.at[i], sems.at[i]).wait()
        parts.append(mm(normed, w_ref[i]).astype(BF16))
    for head in range(HEADS):
        cols = slice(head * HEAD, (head + 1) * HEAD)
        chunk = jnp.concatenate([part[:, cols] for part in parts] + [marks], axis=1)
        for x in range(4):
            chunk_ref[x, HOLDERS[head]] = chunk
    for x in range(4):
        for holder in IDLE:
            chunk_ref[x, holder] = jnp.zeros((SLOTS, 4 * HEAD), BF16)


def embed(scalars, rows, ids, tokens, gain, bias, wk, wv, wq):
    return pl.pallas_call(
        embed_kernel,
        out_shape=(
            jax.ShapeDtypeStruct((4, 16, SLOTS, 4 * HEAD), BF16),
            jax.ShapeDtypeStruct((SLOTS, D), BF16),
            jax.ShapeDtypeStruct((SLOTS, D), F32),
        ),
        in_specs=[SMEM_SPEC] + [VMEM_SPEC] * 5 + [HBM_SPEC] * 3,
        out_specs=(VMEM_SPEC,) * 3,
        scratch_shapes=[pltpu.VMEM((3, D, D), BF16), pltpu.SemaphoreType.DMA((3,))],
        compiler_params=pltpu.CompilerParams(vmem_limit_bytes=58 * 2**20),
        cost_estimate=pl.CostEstimate(
            flops=6 * SLOTS * D * D, bytes_accessed=6 * 2**20, transcendentals=0
        ),
    )(scalars, rows, ids, tokens, gain, bias, wk, wv, wq)


def code_rows(recv_ref, codes_ref):
    lane = lax.broadcasted_iota(jnp.int32, (8, HEAD), 1)
    pick = jnp.where(lane == 0, 1.0, jnp.where(lane == 1, 64.0, 0.0)).astype(BF16)
    for kb in range(8):
        codes = mm_nt(pick, recv_ref[kb % 4, kb // 4, :, 3 * HEAD :])
        row = lax.broadcasted_iota(jnp.int32, (8, RUN), 0)
        codes_ref[kb] = jnp.where((row == 1) & (codes > 0.0), -1.0, codes)


def code_cols(block):
    marks = block[:, 3 * HEAD :].astype(F32)
    return marks[:, 0:1] + 64.0 * marks[:, 1:2]


def attend_kernel(x_ref, recv_ref, out_ref, low_ref, lse_ref, codes_ref):
    x = x_ref[0]
    code_rows(recv_ref, codes_ref)
    for run in range(2):
        q = recv_ref[x, run][:, 2 * HEAD : 3 * HEAD] * SCALE
        last = 4 * run + x
        qcodes = codes_ref[last]

        def block(kb, carry, diagonal):
            peak, total, acc = carry
            kv = recv_ref[lax.rem(kb, 4), kb // 4]
            kcode = code_cols(kv)
            scores = mm_nt(kv[:, :HEAD], q)
            if diagonal:
                rows = lax.broadcasted_iota(jnp.int32, (RUN, RUN), 0)
                cols = lax.broadcasted_iota(jnp.int32, (RUN, RUN), 1)
                allowed = (kcode == qcodes[0:1]) & (rows <= cols)
            else:
                allowed = kcode == qcodes[1:2]
            scores = jnp.where(allowed, scores, NEG_LARGE)
            new_peak = jnp.maximum(peak, jnp.max(scores, axis=0, keepdims=True))
            probs = jnp.exp(scores - new_peak)
            decay = jnp.exp(peak - new_peak)
            total = total * decay + jnp.sum(probs, axis=0, keepdims=True)
            acc = acc * decay + mm_tn(kv[:, HEAD : 2 * HEAD], probs.astype(BF16))
            return new_peak, total, acc

        start = (
            jnp.full((1, RUN), NEG_LARGE, F32),
            jnp.zeros((1, RUN), F32),
            jnp.zeros((HEAD, RUN), F32),
        )
        carry = block(last, start, True)
        peak, total, acc = lax.fori_loop(
            0, last, lambda kb, carry: block(kb, carry, False), carry
        )
        mixed = (acc / total).T
        out_ref[run] = mixed
        low_ref[run, :, :HEAD] = mixed.astype(BF16)
        low_ref[run, :, HEAD:] = jnp.zeros((RUN, HEAD), BF16)
        lse_ref[run] = peak + jnp.log(total)


def attend(x, recv):
    return pl.pallas_call(
        attend_kernel,
        out_shape=(
            jax.ShapeDtypeStruct((2, RUN, HEAD), F32),
            jax.ShapeDtypeStruct((2, RUN, 2 * HEAD), BF16),
            jax.ShapeDtypeStruct((2, 1, RUN), F32),
        ),
        in_specs=[SMEM_SPEC, VMEM_SPEC],
        out_specs=(VMEM_SPEC,) * 3,
        scratch_shapes=[pltpu.VMEM((8, 8, RUN), F32)],
        compiler_params=pltpu.CompilerParams(vmem_limit_bytes=14 * 2**20),
        cost_estimate=pl.CostEstimate(
            flops=24 * 768 * 3072 * 64, bytes_accessed=3 * 2**20, transcendentals=768 * 3072
        ),
    )(x, recv)


def attend_back_kernel(
    x_ref, recv_ref, do_ref, mixed_ref, lse_ref, dq_ref, dkv_ref, codes_ref, acc_ref
):
    x = x_ref[0]
    acc_ref[...] = jnp.zeros_like(acc_ref)
    code_rows(recv_ref, codes_ref)
    for run in range(2):
        q = recv_ref[x, run][:, 2 * HEAD : 3 * HEAD] * SCALE
        do = do_ref[run][:, :HEAD]
        last = 4 * run + x
        qcodes = codes_ref[last]
        lse = lse_ref[run]
        inner = dot(
            jnp.ones((8, HEAD), F32), do.astype(F32) * mixed_ref[run], ((1,), (1,)), EXACT
        )[0:1]

        def block(kb, dq, diagonal):
            kv = recv_ref[lax.rem(kb, 4), kb // 4]
            keys = kv[:, :HEAD]
            kcode = code_cols(kv)
            scores = mm_nt(keys, q)
            if diagonal:
                rows = lax.broadcasted_iota(jnp.int32, (RUN, RUN), 0)
                cols = lax.broadcasted_iota(jnp.int32, (RUN, RUN), 1)
                allowed = (kcode == qcodes[0:1]) & (rows <= cols)
            else:
                allowed = kcode == qcodes[1:2]
            probs = jnp.where(allowed, jnp.exp(scores - lse), 0.0)
            grad_probs = mm_nt(kv[:, HEAD : 2 * HEAD], do)
            grad_raw = (probs * (grad_probs - inner)).astype(BF16)
            dk = mm(grad_raw, q)
            dv = mm(probs.astype(BF16), do)
            acc_ref[kb] += jnp.concatenate([dk, dv], axis=1)
            return dq + mm_tn(keys, grad_raw)

        dq = block(last, jnp.zeros((HEAD, RUN), F32), True)
        dq = lax.fori_loop(0, last, lambda kb, carry: block(kb, carry, False), dq)
        dq_ref[run] = (dq * SCALE).T.astype(BF16)
    for kb in range(8):
        dkv_ref[kb % 4, kb // 4] = acc_ref[kb].astype(BF16)


def attend_back(x, recv, do, mixed, lse):
    return pl.pallas_call(
        attend_back_kernel,
        out_shape=(
            jax.ShapeDtypeStruct((2, RUN, HEAD), BF16),
            jax.ShapeDtypeStruct((4, 2, RUN, 2 * HEAD), BF16),
        ),
        in_specs=[SMEM_SPEC] + [VMEM_SPEC] * 4,
        out_specs=(VMEM_SPEC,) * 2,
        scratch_shapes=[pltpu.VMEM((8, 8, RUN), F32), pltpu.VMEM((8, RUN, 2 * HEAD), F32)],
        compiler_params=pltpu.CompilerParams(vmem_limit_bytes=18 * 2**20),
        cost_estimate=pl.CostEstimate(
            flops=60 * 768 * 3072 * 64, bytes_accessed=6 * 2**20, transcendentals=768 * 3072
        ),
    )(x, recv, do, mixed, lse)


ROOT = 0.7978845608028654
CUBE = 0.044715


def feed_kernel(
    parts_ref, routed_ref, gate_ref, branch_ref, low_ref, grad_act_ref, gain_ref, bias_ref,
    core_ref, wo_hbm, we_hbm,
    kept_ref, given_ref, back_ref, projected_ref, hidden_ref, logit_ref, vector_ref, act_ref,
    wo_ref, we_ref, sems,
):
    copies = [pltpu.make_async_copy(wo_hbm, wo_ref, sems.at[4])]
    for i in range(4):
        cols = pl.ds(i * D, D)
        copies.append(pltpu.make_async_copy(we_hbm.at[:, cols], we_ref.at[i], sems.at[i]))
    for copy in copies:
        copy.start()
    mixed = jnp.concatenate([parts_ref[holder, :, :HEAD] for holder in HOLDERS], axis=1)
    copies[0].wait()
    projected = mm(mixed, wo_ref[...])
    projected_ref[...] = projected
    routed = routed_ref[...]
    gain = gain_ref[...]
    normed, unit, inv = layer_norm(routed + projected, gain, bias_ref[...])
    normed = normed.astype(BF16)
    grad_branch = branch_ref[...]
    grad_contracted = low_ref[...]
    grad_normed = jnp.zeros((SLOTS, D), F32)
    inner = jnp.sum(grad_branch * projected, axis=1, keepdims=True)
    for i in range(4):
        copies[i + 1].wait()
        v = mm(normed, we_ref[i])
        t = jnp.tanh(ROOT * (v + CUBE * v * v * v))
        half = 0.5 * (1.0 + t)
        act = v * half
        slope = half + 0.5 * v * (1.0 - t * t) * (ROOT * (1.0 + 3.0 * CUBE * v * v))
        grad_act = grad_act_ref[:, i * D : (i + 1) * D]
        inner += jnp.sum(act * grad_act, axis=1, keepdims=True)
        act = act.astype(BF16)
        grad_expanded = (grad_act * slope).astype(BF16)
        grad_normed += mm_nt(grad_expanded, we_ref[i])
        act_ref[:, i * D : (i + 1) * D] = act

        @pl.when(core_ref[0] == 0)
        def _(i=i, grad_expanded=grad_expanded, act=act):
            kept_ref[i, :, :D] = normed
            kept_ref[i, :, D : 2 * D] = grad_expanded
            given_ref[i, :, :D] = act
            given_ref[i, :, D : 2 * D] = grad_contracted

        @pl.when(core_ref[0] == 1)
        def _(i=i, grad_expanded=grad_expanded, act=act):
            given_ref[i, :, :D] = normed
            given_ref[i, :, D : 2 * D] = grad_expanded
            kept_ref[i, :, :D] = act
            kept_ref[i, :, D : 2 * D] = grad_contracted
    grad_logit = (1.0 - gate_ref[...]) * inner
    logit_ref[...] = grad_logit
    grad_hidden = layer_norm_back(grad_normed, unit, inv, gain)
    hidden_ref[...] = grad_hidden
    grad_projected = (grad_branch + grad_hidden).astype(BF16)
    grad_mixed = mm_nt(grad_projected, wo_ref[...]).astype(BF16)
    for head in range(HEADS):
        back_ref[HOLDERS[head], :, :HEAD] = grad_mixed[:, head * HEAD : (head + 1) * HEAD]
        back_ref[HOLDERS[head], :, HEAD:] = jnp.zeros((SLOTS, HEAD), BF16)
    for holder in IDLE:
        back_ref[holder] = jnp.zeros((SLOTS, 2 * HEAD), BF16)
    halves = (mixed[:, :384], mixed[:, 384:])
    for i in range(4):
        part = grad_projected[:, i * 192 : (i + 1) * 192]
        kept_ref[i, :, 2 * D + 384 :] = part
        given_ref[i, :, 2 * D + 384 :] = part
    for core in range(2):

        @pl.when(core_ref[0] == core)
        def _(core=core):
            for i in range(4):
                kept_ref[i, :, 2 * D : 2 * D + 384] = halves[core]
                given_ref[i, :, 2 * D : 2 * D + 384] = halves[1 - core]

    vector_ref[0:1] = jnp.sum(grad_logit * routed, axis=0, keepdims=True)
    vector_ref[1:2] = jnp.sum(grad_normed * unit, axis=0, keepdims=True)
    vector_ref[2:3] = jnp.sum(grad_normed, axis=0, keepdims=True)


def feed(parts, routed, gate, branch, low, grad_act, gain, bias, core, wo, we):
    return pl.pallas_call(
        feed_kernel,
        out_shape=(
            jax.ShapeDtypeStruct((4, SLOTS, 2 * D + 576), BF16),
            jax.ShapeDtypeStruct((4, SLOTS, 2 * D + 576), BF16),
            jax.ShapeDtypeStruct((16, SLOTS, 2 * HEAD), BF16),
            jax.ShapeDtypeStruct((SLOTS, D), F32),
            jax.ShapeDtypeStruct((SLOTS, D), F32),
            jax.ShapeDtypeStruct((SLOTS, 1), F32),
            jax.ShapeDtypeStruct((3, D), F32),
            jax.ShapeDtypeStruct((SLOTS, FF), BF16),
        ),
        in_specs=[VMEM_SPEC] * 8 + [SMEM_SPEC] + [HBM_SPEC] * 2,
        out_specs=(VMEM_SPEC,) * 8,
        scratch_shapes=[
            pltpu.VMEM((D, D), BF16),
            pltpu.VMEM((4, D, D), BF16),
            pltpu.SemaphoreType.DMA((5,)),
        ],
        compiler_params=pltpu.CompilerParams(vmem_limit_bytes=58 * 2**20),
        cost_estimate=pl.CostEstimate(
            flops=20 * SLOTS * D * D, bytes_accessed=10 * 2**20, transcendentals=SLOTS * FF
        ),
    )(parts, routed, gate, branch, low, grad_act, gain, bias, core, wo, we)


def unit_kernel(*refs):
    parts, (vector_ref, out_ref) = refs[:4], refs[4:]

    def outer(left, right):
        total = jnp.zeros((left.stop - left.start, right.stop - right.start), F32)
        for part in parts:
            total += mm_tn(part[:, left], part[:, right])
        return total.astype(BF16)

    tile = outer(slice(2 * D, 2 * D + 384), slice(2 * D + 384, 2 * D + 576))
    for block in range(2):
        unit = outer(slice(block * 384, (block + 1) * 384), slice(D, 2 * D))
        for i in range(8):
            at = block * 8 + i
            out_ref[at // 4, at % 4, :, :D] = unit[i * 48 : (i + 1) * 48]
            out_ref[at // 4, at % 4, :, D:] = jnp.concatenate(
                [
                    tile[(at // 2) * 48 : (at // 2 + 1) * 48, (at % 2) * 96 : (at % 2 + 1) * 96],
                    vector_ref[at],
                ],
                axis=1,
            )


def unit_grads(parts, vectors):
    return pl.pallas_call(
        unit_kernel,
        out_shape=jax.ShapeDtypeStruct((4, 4, 48, 896), BF16),
        in_specs=[VMEM_SPEC] * 5,
        out_specs=VMEM_SPEC,
        compiler_params=pltpu.CompilerParams(vmem_limit_bytes=14 * 2**20),
        cost_estimate=pl.CostEstimate(
            flops=2 * 384 * D * D, bytes_accessed=3 * 2**20, transcendentals=0
        ),
    )(*parts, vectors)


def embed_back_kernel(
    back_ref, routed_ref, hidden_ref, logit_ref, rows_ref, grad_ref, router_ref, gain_ref,
    wk_hbm, wv_hbm, wq_hbm, out_ref, w_ref, sems,
):
    copies = [
        pltpu.make_async_copy(w, w_ref.at[i], sems.at[i])
        for i, w in enumerate((wk_hbm, wv_hbm, wq_hbm))
    ]
    for copy in copies:
        copy.start()
    routed = routed_ref[...]
    gain = gain_ref[...].reshape(1, D)
    unused, unit, inv = layer_norm(routed, gain, 0.0)
    grad_normed = jnp.zeros((SLOTS, D), F32)
    for i in range(3):
        grads = jnp.concatenate(
            [back_ref[holder, :, i * HEAD : (i + 1) * HEAD] for holder in HOLDERS], axis=1
        )
        copies[i].wait()
        grad_normed += mm_nt(grads, w_ref[i])
    grad_rows = (
        logit_ref[...] * router_ref[...].reshape(1, D)
        + hidden_ref[...]
        + layer_norm_back(grad_normed, unit, inv, gain)
    )
    places = lax.broadcasted_iota(jnp.int32, (TOK, SLOTS), 0)
    picks = (rows_ref[...] == places).astype(F32)
    out_ref[...] = (
        grad_ref[...].astype(F32) + dot(picks, grad_rows, ((1,), (0,)), EXACT)
    ).astype(BF16)


def embed_back(back, routed, hidden, logit, rows, grad, router, gain, wk, wv, wq):
    return pl.pallas_call(
        embed_back_kernel,
        out_shape=jax.ShapeDtypeStruct((TOK, D), BF16),
        in_specs=[VMEM_SPEC] * 8 + [HBM_SPEC] * 3,
        out_specs=VMEM_SPEC,
        scratch_shapes=[pltpu.VMEM((3, D, D), BF16), pltpu.SemaphoreType.DMA((3,))],
        compiler_params=pltpu.CompilerParams(vmem_limit_bytes=58 * 2**20),
        cost_estimate=pl.CostEstimate(
            flops=6 * SLOTS * D * D, bytes_accessed=6 * 2**20, transcendentals=0
        ),
    )(back, routed, hidden, logit, rows, grad, router, gain, wk, wv, wq)


def body(
    tokens,
    router,
    gain_one,
    bias_one,
    w_query,
    w_key,
    w_value,
    w_out,
    gain_two,
    bias_two,
    w_expand,
    w_contract,
    cotangent,
    seq_ids,
    routed_rows,
    routed_count,
):
    x_at = lax.axis_index("x").astype(jnp.int32)
    core_at = lax.axis_index("c").astype(jnp.int32)
    y_at = lax.axis_index(("yh", "yl")).astype(jnp.int32)
    z_at = lax.axis_index("z").astype(jnp.int32)
    first_at = jnp.where(core_at == 0, x_at, z_at)
    second_at = jnp.where(core_at == 0, z_at, x_at)
    row_index = routed_rows[0, 0]
    routed_total = routed_count[0, 0]
    x_local = tokens[0]
    place_at = lax.axis_index(("z", "c")).astype(jnp.int32)
    to_heads, normed_low, routed_x = embed(
        jnp.stack([routed_total, place_at]),
        routed_rows[0],
        seq_ids,
        x_local,
        gain_one,
        bias_one,
        w_key,
        w_value,
        w_query,
    )
    recv = swap(to_heads.reshape(64, SLOTS, 4 * HEAD), ("x",) + SIXTEEN)
    w_part = jnp.concatenate(
        [
            lax.dynamic_slice(
                w,
                (lax.axis_index(("x", "z", "yl")) * 24, (core_at * 2 + lax.axis_index("yh")) * 3 * HEAD),
                (24, 3 * HEAD),
            )
            for w in (w_key, w_value, w_query)
        ],
        axis=1,
    ).astype(F32)
    recv, w_part = lax.optimization_barrier((recv, w_part))
    recv = recv.reshape(4, 2, RUN, 4 * HEAD)
    normed_block = lax.all_gather(normed_low, SIXTEEN, axis=0, tiled=True)

    is_valid = jnp.arange(SLOTS, dtype=jnp.int32) < routed_total
    picks = row_index[:, None] == jnp.arange(TOK, dtype=jnp.int32)[None, :]
    pick_low = picks.astype(BF16)
    pick_full = picks.astype(F32)
    gate_value = jax.nn.sigmoid(jnp.sum(routed_x * router[None, :], axis=-1))
    gate_used = jnp.where(is_valid, gate_value, 0.0)
    grad_local = cotangent[0]
    grad_branch = gate_used[:, None] * mm(pick_low, grad_local)
    grad_contracted = grad_branch.astype(BF16)
    grad_activated = mm_nt(grad_contracted, w_contract)

    mixed_here, mixed_low, lse = attend(x_at[None], recv)
    mixed_parts = swap(mixed_low.reshape(16, SLOTS, 2 * HEAD), SIXTEEN)
    (kept, given, do_parts, projected, grad_hidden, grad_logit, vectors, activated_low) = feed(
        mixed_parts,
        routed_x,
        gate_value[:, None],
        grad_branch,
        grad_contracted,
        grad_activated,
        gain_two[None],
        bias_two[None],
        core_at[None],
        w_out,
        w_expand,
    )
    given = lax.ppermute(given, "c", [(0, 1), (1, 0)])
    eight = jnp.concatenate([kept, given], axis=1)
    eight = ring_swap(eight, first_at, lambda step: ring_pairs(0, step), CUBE_AXES)
    do_parts = swap(do_parts, SIXTEEN)
    eight, do_parts, normed_block = lax.optimization_barrier((eight, do_parts, normed_block))
    vectors = jnp.pad(vectors.astype(BF16).reshape(16, 48, 3), ((0, 0), (0, 0), (0, 29)))
    partial_grads = unit_grads(eight, vectors)
    do_parts, partial_grads = lax.optimization_barrier((do_parts, partial_grads))
    grad_q, grad_kv = attend_back(
        x_at[None], recv, do_parts.reshape(2, RUN, 2 * HEAD), mixed_here, lse
    )
    partial_grads = ring_swap(
        partial_grads, second_at, lambda step: ring_pairs(1, step), CUBE_AXES
    )
    partial_grads, grad_kv = lax.optimization_barrier((partial_grads, grad_kv))
    partial_grads = sum(part.astype(F32) for part in partial_grads).astype(BF16)
    partial_grads = ring_swap(
        partial_grads,
        y_at,
        lambda step: [(i, (i + step) % 4) for i in range(4)],
        ("yh", "yl"),
    )
    own_grads = sum(part.astype(F32) for part in partial_grads).astype(BF16)
    grad_kv, own_grads = lax.optimization_barrier((grad_kv, own_grads))
    grad_kv = swap(grad_kv, ("x",))
    grad_kv_sum = jnp.sum(grad_kv.astype(F32), axis=0).astype(BF16)
    grad_heads = jnp.concatenate(
        [grad_kv_sum.reshape(2 * RUN, 2 * HEAD), grad_q.reshape(2 * RUN, HEAD)], axis=1
    )
    units = lax.all_gather(own_grads, CHIPS, axis=0, tiled=False)
    branch = projected + mm(activated_low, w_contract)
    output = (
        x_local.astype(F32)
        + dot(pick_full, gate_used[:, None] * branch, ((0,), (0,)), EXACT)
    ).astype(BF16)

    grad_qkv = mm_tn(normed_block, grad_heads).astype(BF16).reshape(32, 24, 3 * HEAD)
    column_sum = jnp.sum(grad_heads.astype(F32), axis=0).astype(BF16)
    column_sum = jnp.broadcast_to(column_sum[None, None, :], (32, 8, 3 * HEAD))
    grad_qkv = swap(jnp.concatenate([grad_qkv, column_sum], axis=1), ("x", "z", "yl"))
    grad_qkv, output = lax.optimization_barrier((grad_qkv, output))
    grad_qkv = jnp.sum(grad_qkv.reshape(4, 4, 2, 32, 3 * HEAD)[:, :3].astype(F32), axis=(0, 2))
    grad_qkv = jnp.concatenate(
        [
            grad_qkv[:, :, kind * HEAD : (kind + 1) * HEAD].transpose(1, 0, 2).reshape(32, 3 * HEAD)
            for kind in range(3)
        ],
        axis=1,
    )
    column_sum = grad_qkv[24]
    grad_qkv = grad_qkv[:24]
    norm_sums = jnp.stack(
        [jnp.sum(w_part * grad_qkv, axis=1), jnp.sum(w_part * column_sum[None, :], axis=1)], axis=1
    )
    own_qkv = jnp.concatenate([grad_qkv, jnp.pad(norm_sums, ((0, 0), (0, 62)))], axis=1)
    own_qkv = own_qkv.astype(BF16)
    heads = spread(own_qkv, ("yh", "yl", "z"))
    heads, grad_heads = lax.optimization_barrier((heads, grad_heads))
    heads = [heads] + [
        lax.ppermute(heads, "x", [((i + step) % 4, i) for i in range(4)]) for step in (1, 2, 3)
    ]
    back = swap(
        jnp.pad(grad_heads, ((0, 0), (0, HEAD))).reshape(16, SLOTS, 4 * HEAD), SIXTEEN
    )
    input_grad = embed_back(
        back,
        routed_x,
        grad_hidden,
        grad_logit,
        routed_rows[0],
        grad_local,
        router,
        gain_one,
        w_key,
        w_value,
        w_query,
    )
    heads, input_grad = lax.optimization_barrier((heads, input_grad))
    heads = heads + other_core(heads)
    units, heads = lax.optimization_barrier((units, heads))
    me = jnp.stack([x_at, y_at, z_at, core_at])
    first = place(me, [units] + heads[:4])
    placed = place(me, other_core([units]) + heads[4:], first)
    final_expand, final_contract, final_out, final_key, final_value, final_query = placed[:6]
    norm_sums = (first[6][:, :2] + placed[6][:, :2]).T
    grad_gain_one = (norm_sums[0] - bias_one * norm_sums[1]) / gain_one
    grad_bias_one = norm_sums[1]
    vectors = first[7][:, :, 96:] + placed[7][:, :, 96:]
    vectors = vectors[:, :, :3].reshape(3, D)
    return (
        output[None],
        input_grad[None],
        vectors[0],
        grad_gain_one,
        grad_bias_one,
        final_query,
        final_key,
        final_value,
        final_out,
        vectors[1],
        vectors[2],
        final_expand,
        final_contract,
    )


def solution(mesh):
    fine = Mesh(mesh.devices.reshape(2, 4, 4, 2, 2), ("yh", "x", "z", "c", "yl"))
    seq = ("yh", "x", "z", "c")
    in_specs = (
        (P("yl", seq, None),)
        + (P(),) * 11
        + (P("yl", seq, None), P("yl", seq), P("yl", seq, None), P("yl", seq))
    )
    out_specs = (P("yl", seq, None),) * 2 + (P(),) * 11
    return jax.shard_map(body, mesh=fine, in_specs=in_specs, out_specs=out_specs, check_vma=False)
```

profile of v0, /device:TPU:1, one launch (start us, length us, event | category | flops | bytes accessed | tf_op | source)
XLA Modules:
  0.0 247.0 jit_solution(14920381264177634500)
XLA Ops:
  8.4 4.7 %shard_map.255 = (bf16[4,16,48,256]{3,2,1,0:T(8,128)(2,1)}, bf16[48,768]{1,0:T(8,128)(2,1)}, f32[48,768]{1,0:T(8,128)}) custom-call(s32[2]{0:T(128)} %pad_add_fusion.count_ref, s32[1,48]{1,0:T(1,128)} %bitcast.92, s32[1,256]{1,0:T(1,128)} %ids_ref.1, bf16[256,768]{1,0:T(8,128)(2,1)} %bitcast.84, f32[768]{0:T(1024)} %gain_ref.3, f32[768]{0:T(1024)} %bias_ref.1, ...), custom_call_target="tpu_custom_call" | custom-call | flops 169869312 | bytes 6291456 | tf_op jit(solution)/shard_map/pallas_call | solution.py:319
  13.1 12.6 %all-to-all-start = ((bf16[64,48,256]{2,1,0:T(8,128)(2,1)}), bf16[64,48,256]{2,1,0:T(8,128)(2,1)S(1)}, u32[]{:S(2)}, u32[]{:S(2)}) async-start(bf16[64,48,256]{2,1,0:T(8,128)(2,1)} %bitcast.83), calls=%async_computation | async-start | bytes 3145728 | tf_op jit(solution)/shard_map/all_to_all | solution.py:41
  26.5 0.8 dynamic_slice.50
  27.3 0.8 dynamic_slice.48
  28.1 0.8 dynamic_slice.49
  29.2 0.9 fusion.11
  30.1 20.7 %all-to-all-done = bf16[64,48,256]{2,1,0:T(8,128)(2,1)S(1)} async-done(((bf16[64,48,256]{2,1,0:T(8,128)(2,1)}), bf16[64,48,256]{2,1,0:T(8,128)(2,1)S(1)}, u32[]{:S(2)}, u32[]{:S(2)}) %all-to-all-start) | async-done | bytes 1572896 | tf_op jit(solution)/shard_map/all_to_all | solution.py:41
  50.8 4.5 %shard_map.256 = (f32[2,384,64]{2,1,0:T(8,128)S(1)}, bf16[2,384,128]{2,1,0:T(8,128)(2,1)}, f32[2,1,384]{2,1,0:T(1,128)S(1)}) custom-call(s32[1]{0:T(128)} %bitcast.x_ref, bf16[4,2,384,256]{3,2,1,0:T(8,128)(2,1)S(1)} %bitcast.78), custom_call_target="tpu_custom_call" | custom-call | flops 3623878656 | bytes 3145728 | tf_op jit(solution)/shard_map/pallas_call | solution.py:394
  56.0 3.5 %all-to-all-start.1 = ((bf16[16,48,128]{2,1,0:T(8,128)(2,1)}), bf16[16,48,128]{2,1,0:T(8,128)(2,1)S(1)}, u32[]{:S(2)}, u32[]{:S(2)}) async-start(bf16[16,48,128]{2,1,0:T(8,128)(2,1)} %bitcast.7), calls=%async_computation.1 | async-start | bytes 393216 | tf_op jit(solution)/shard_map/all_to_all | solution.py:41
  59.6 4.6 %fusion.12.grad_act_ref = f32[48,3072]{1,0:T(8,128)} fusion(bf16[48,768]{1,0:T(8,128)(2,1)S(1)} %get-tuple-element.172.low_ref, bf16[3072,768]{1,0:T(8,128)(2,1)} %param.27), kind=kOutput, calls=%fused_computation.61 | convolution fusion | flops 226492416 | bytes 5382144 | tf_op jit(solution)/shard_map/dot_general | solution.py:119
  66.1 1.7 all-to-all-done.1.parts_ref
  68.4 8.3 %shard_map.257 = (bf16[4,48,2112]{2,1,0:T(8,128)(2,1)}, bf16[4,48,2112]{2,1,0:T(8,128)(2,1)}, bf16[16,48,128]{2,1,0:T(8,128)(2,1)}, f32[48,768]{1,0:T(8,128)}, f...) custom-call(bf16[16,48,128]{2,1,0:T(8,128)(2,1)} %copy-done.10, ...), custom_call_target="tpu_custom_call" | custom-call | flops 566231040 | bytes 10485760 | tf_op jit(solution)/shard_map/pallas_call | solution.py:555
  76.7 0.9 collective-permute-start
  77.7 1.2 constant_dynamic-update-slice_fusion.1
  78.9 1.0 collective-permute-done
  80.0 1.1 dynamic-slice_bitcast_fusion
  81.0 1.4 collective-permute-start.3
  83.0 9.8 %all-to-all-start.2 = ((bf16[16,48,128]{2,1,0:T(8,128)(2,1)}), bf16[16,48,128]{2,1,0:T(8,128)(2,1)}, u32[]{:S(2)}, u32[]{:S(2)}) async-start(bf16[16,48,128]{2,1,0:T(8,128)(2,1)} %get-tuple-element.86), calls=%async_computation.2 | async-start | bytes 393216 | tf_op jit(solution)/shard_map/all_to_all | solution.py:41
  92.9 1.0 reshape.120
  93.9 1.0 pad.13.refs_4_
  94.9 6.2 %all-to-all-done.2 = bf16[16,48,128]{2,1,0:T(8,128)(2,1)} async-done(((bf16[16,48,128]{2,1,0:T(8,128)(2,1)}), bf16[16,48,128]{2,1,0:T(8,128)(2,1)}, u32[]{:S(2)}, u32[]{:S(2)}) %all-to-all-start.2) | async-done | bytes 196640 | tf_op jit(solution)/shard_map/all_to_all | solution.py:41
  101.2 1.7 shard_map.258
  103.0 2.4 collective-permute-start.6
  105.4 2.0 collective-permute-start.5
  107.4 5.9 %shard_map.259 = (bf16[2,384,64]{2,1,0:T(8,128)(2,1)S(1)}, bf16[4,2,384,128]{3,2,1,0:T(8,128)(2,1)S(1)}) custom-call(s32[1]{0:T(128)} %bitcast.x_ref, bf16[4,2,384,256]{3,2,1,0:T(8,128)(2,1)S(1)} %bitcast.79, bf16[2,384,128]{2,1,0:T(8,128)(2,1)} %bitcast.21.do_ref, f32[2,384,64]{2,1,0:T(8,128)S(1)} %copy-done.6, f32[2,1,384]{2,1,0:T(1,128)S(1)} %get-tuple-element.98.lse_ref), custom_call_target="tpu_custom_call" | custom-call | flops 9059696640 | bytes 6291456 | tf_op jit(solution)/shard_map/pallas_call | solution.py:454
  113.3 3.6 %collective-permute-done.4 = bf16[4,48,896]{2,1,0:T(8,128)(2,1)S(1)} collective-permute-done((bf16[4,48,896]{2,1,0:T(8,128)(2,1)S(1)}, bf16[4,48,896]{2,1,0:T(8,128)(2,1)S(1)}, u32[]{:S(2)}, u32[]{:S(2)}) %collective-permute-start.4) | collective-permute-done | bytes 344096 | tf_op jit(solution)/shard_map/ppermute | solution.py:76
  117.6 2.4 collective-permute-start.9
  119.9 1.9 collective-permute-done.7
  121.8 2.9 %collective-permute-done.8 = bf16[48,896]{1,0:T(8,128)(2,1)S(1)} collective-permute-done((bf16[48,896]{1,0:T(8,128)(2,1)S(1)}, bf16[48,896]{1,0:T(8,128)(2,1)S(1)}, u32[]{:S(2)}, u32[]{:S(2)}) %collective-permute-start.8) | collective-permute-done | bytes 86048 | tf_op jit(solution)/shard_map/ppermute | solution.py:76
  125.5 16.9 %all_to_all.35 = bf16[4,2,384,128]{3,2,1,0:T(8,128)(2,1)S(1)} all-to-all(bf16[4,2,384,128]{3,2,1,0:T(8,128)(2,1)S(1)} %get-tuple-element.105), channel_id=1, replica_groups=mesh['yh'=2,'x'=4,'z'=4,'c'=2,'yl'=2] {'x'}, dimensions={0} | all-to-all | bytes 1572864 | tf_op jit(solution)/shard_map/all_to_all | solution.py:41
  142.6 1.7 convolution_convert_fusion
  144.7 0.9 pad_maximum_fusion
  145.6 3.9 %all-to-all-start.4 = ((bf16[32,32,192]{2,1,0:T(8,128)(2,1)}), bf16[32,32,192]{2,1,0:T(8,128)(2,1)S(1)}, u32[]{:S(2)}, u32[]{:S(2)}) async-start(bf16[32,32,192]{2,1,0:T(8,128)(2,1)} %pad_maximum_fusion), calls=%async_computation.4 | async-start | bytes 1048576 | tf_op jit(solution)/shard_map/all_to_all | solution.py:41
  149.5 3.3 %fusion.1 = f32[48,768]{1,0:T(8,128)S(1)} fusion(f32[48,768]{1,0:T(8,128)S(1)} %copy-done.13, bf16[48,3072]{1,0:T(8,128)(2,1)S(1)} %copy-done.12, bf16[3072,768]{1,0:T(8,128)(2,1)} %param.27, f32[48]{0:T(128)S(1)} %get-tuple-element.154), kind=kOutput, calls=%fused_computation.4 | convolution fusion | flops 226566144 | bytes 5308608 | tf_op jit(solution)/shard_map/dot_general | solution.py:119
  152.8 1.3 fusion
  154.1 5.2 %all-to-all-done.4 = bf16[32,32,192]{2,1,0:T(8,128)(2,1)S(1)} async-done(((bf16[32,32,192]{2,1,0:T(8,128)(2,1)}), bf16[32,32,192]{2,1,0:T(8,128)(2,1)S(1)}, u32[]{:S(2)}, u32[]{:S(2)}) %all-to-all-start.4) | async-done | bytes 393248 | tf_op jit(solution)/shard_map/all_to_all | solution.py:41
  160.5 12.8 %all_to_all.36.refs_1_ = bf16[16,24,640]{2,1,0:T(8,128)(2,1)S(1)} all-to-all(bf16[16,24,640]{2,1,0:T(8,128)(2,1)S(1)} %broadcast_in_dim.47), channel_id=1, replica_groups=mesh['yh'=2,'x'=4,'z'=4,'c'=2,'yl'=2] {'yh','yl','z'}, dimensions={0} | all-to-all | bytes 983040 | tf_op jit(solution)/shard_map/all_to_all | solution.py:41
  173.8 1.8 collective-permute-start.11
  175.6 1.2 collective-permute-start.10
  176.9 22.3 %all_to_all.37.back_ref = bf16[16,48,256]{2,1,0:T(8,128)(2,1)} all-to-all(bf16[16,48,256]{2,1,0:T(8,128)(2,1)S(1)} %bitcast.85), channel_id=1, replica_groups=mesh['yh'=2,'x'=4,'z'=4,'c'=2,'yl'=2] {'yh','z','c'}, dimensions={0} | all-to-all | bytes 786432 | tf_op jit(solution)/shard_map/all_to_all | solution.py:41
  199.2 6.1 %shard_map.260 = bf16[256,768]{1,0:T(8,128)(2,1)} custom-call(bf16[16,48,256]{2,1,0:T(8,128)(2,1)} %all_to_all.37.back_ref, f32[48,768]{1,0:T(8,128)} %get-tuple-element.83.routed_ref, f32[48,768]{1,0:T(8,128)} %get-tuple-element.114.hidden_ref, f32[48,1]{1,0:T(8,128)} %get-tuple-element.115.logit_ref, s32[1,48]{1,0:T(1,128)} %bitcast.93, ...), custom_call_target="tpu_custom_call" | custom-call | flops 169869312 | bytes 6291456 | tf_op jit(solution)/shard_map/pallas_call | solution.py:651
  205.3 2.6 %collective-permute-done.10.refs_2_ = bf16[16,24,640]{2,1,0:T(8,128)(2,1)S(1)} collective-permute-done((bf16[16,24,640]{2,1,0:T(8,128)(2,1)S(1)}, bf16[16,24,640]{2,1,0:T(8,128)(2,1)S(1)}, u32[]{:S(2)}, u32[]{:S(2)}) %collective-permute-start.10) | collective-permute-done | bytes 491552 | tf_op jit(solution)/shard_map/ppermute | solution.py:804
  208.0 6.0 %collective-permute-start.13 = (bf16[16,24,640]{2,1,0:T(8,128)(2,1)S(1)}, bf16[16,24,640]{2,1,0:T(8,128)(2,1)S(1)}, u32[]{:S(2)}, u32[]{:S(2)}) collective-permute-start(bf16[16,24,640]{2,1,0:T(8,128)(2,1)S(1)} %all_to_all.36.refs_1_), channel_id=1, source_target_pairs={{0,2},{2,0},{1,3},{3,1},{4,6},{6,4},{5,7},{7,5},{8,10},{10,8},{9,1... | collective-permute-start | bytes 1474568 | tf_op jit(solution)/shard_map/ppermute | solution.py:103
  214.0 0.8 copy-done.1
  218.1 2.6 %copy-done = bf16[3072,896]{1,0:T(8,128)(2,1)S(1)} copy-done((bf16[3072,896]{1,0:T(8,128)(2,1)S(1)}, bf16[3072,896]{1,0:T(8,128)(2,1)}, u32[]{:S(2)}) %copy-start) | copy-done | bytes 5505048
  220.6 1.0 copy-done.2
  221.7 7.7 %shard_map.261 = (f32[768,3072]{1,0:T(8,128)}, f32[3072,768]{1,0:T(8,128)}, f32[768,768]{1,0:T(8,128)}, f32[768,768]{1,0:T(8,128)}, f32[768,768]{1,0:T(8,128)}, ...) custom-call(s32[4]{0:T(128)S(1)} %pad_add_fusion.1.me_ref, ...), custom_call_target="tpu_custom_call" | custom-call | bytes 20971520 | tf_op jit(solution)/shard_map/pallas_call | solution.py:244
  229.5 7.9 %shard_map.262 = (f32[768,3072]{1,0:T(8,128)}, f32[3072,768]{1,0:T(8,128)}, f32[768,768]{1,0:T(8,128)}, f32[768,768]{1,0:T(8,128)}, f32[768,768]{1,0:T(8,128)}, ...) custom-call(s32[4]{0:T(128)S(1)} %pad_add_fusion.1.me_ref, ...), custom_call_target="tpu_custom_call", output_to_operand_aliasing={{0}: (6, {}), {1}: (7, {}), {2}: (8, {}), {3}: (9, {}), {4}... | custom-call | bytes 20971520 | tf_op jit(solution)/shard_map/pallas_call | solution.py:244
  (113 shorter events, 15.4 us)
Async XLA Ops:
  13.1 15.9 %copy-start.9 = (f32[48,768]{1,0:T(8,128)S(1)}, f32[48,768]{1,0:T(8,128)}, u32[]{:S(2)}) copy-start(f32[48,768]{1,0:T(8,128)} %get-tuple-element.83.routed_ref) | copy-start | bytes 442372
  13.1 15.9 %copy-start.17 = (f32[768]{0:T(1024)S(1)}, f32[768]{0:T(1024)}, u32[]{:S(2)}) copy-start(f32[768]{0:T(1024)} %router_ref.1) | copy-start | bytes 9220
  13.1 16.0 %copy-start.8 = (bf16[1,256,768]{2,1,0:T(8,128)(2,1)S(1)}, bf16[1,256,768]{2,1,0:T(8,128)(2,1)}, u32[]{:S(2)}) copy-start(bf16[1,256,768]{2,1,0:T(8,128)(2,1)} %param.28) | copy-start | bytes 1179652
  13.1 16.0 %copy-start.19 = (s32[1,1,48]{2,1,0:T(1,128)S(1)}, s32[1,1,48]{2,1,0:T(1,128)}, u32[]{:S(2)}) copy-start(s32[1,1,48]{2,1,0:T(1,128)} %param.30) | copy-start | bytes 580
  13.1 37.6 %all-to-all-start = ((bf16[64,48,256]{2,1,0:T(8,128)(2,1)}), bf16[64,48,256]{2,1,0:T(8,128)(2,1)S(1)}, u32[]{:S(2)}, u32[]{:S(2)}) async-start(bf16[64,48,256]{2,1,0:T(8,128)(2,1)} %bitcast.83), calls=%async_computation | async-start | bytes 3145728 | tf_op jit(solution)/shard_map/all_to_all | solution.py:41
  25.8 75.4 %all-gather.4.cloned.1.call-start = ((), (), s32[]{:S(2)}) async-start(), calls=%async_computation.7 | async-start | bytes 1253376 | tf_op jit(solution)/shard_map/all_gather | solution.py:717
  30.1 29.5 %copy-start.11 = (bf16[48,768]{1,0:T(8,128)(2,1)}, bf16[48,768]{1,0:T(8,128)(2,1)S(1)}, u32[]{:S(2)}) copy-start(bf16[48,768]{1,0:T(8,128)(2,1)S(1)} %get-tuple-element.172.low_ref) | copy-start | bytes 221188
  55.3 0.7 copy-start.5
  56.0 11.8 %all-to-all-start.1 = ((bf16[16,48,128]{2,1,0:T(8,128)(2,1)}), bf16[16,48,128]{2,1,0:T(8,128)(2,1)S(1)}, u32[]{:S(2)}, u32[]{:S(2)}) async-start(bf16[16,48,128]{2,1,0:T(8,128)(2,1)} %bitcast.7), calls=%async_computation.1 | async-start | bytes 393216 | tf_op jit(solution)/shard_map/all_to_all | solution.py:41
  59.5 4.7 %copy-start.20 = (f32[768]{0:T(1024)S(1)}, f32[768]{0:T(1024)}, u32[]{:S(2)}) copy-start(f32[768]{0:T(1024)} %param.24) | copy-start | bytes 9220
  59.5 5.2 %copy-start.21 = (f32[768]{0:T(1024)S(1)}, f32[768]{0:T(1024)}, u32[]{:S(2)}) copy-start(f32[768]{0:T(1024)} %param.25) | copy-start | bytes 9220
  67.8 0.7 copy-start.10
  76.7 3.1 %collective-permute-start = (bf16[4,48,2112]{2,1,0:T(8,128)(2,1)}, bf16[4,48,2112]{2,1,0:T(8,128)(2,1)S(1)}, u32[]{:S(2)}, u32[]{:S(2)}) collective-permute-start(bf16[4,48,2112]{2,1,0:T(8,128)(2,1)} %get-tuple-element.85), channel_id=1, source_target_pairs={{0,2},{2,0},{1,3},{3,1},{4,6},{6,4},{5,7},{7,5},{8,10},{10,8},{9,1... | collective-permute-start | bytes 2433032 | tf_op jit(solution)/shard_map/ppermute | solution.py:745
  78.9 14.0 %copy-start.18 = (f32[3,768]{1,0:T(4,128)S(1)}, f32[3,768]{1,0:T(4,128)}, u32[]{:S(2)}) copy-start(f32[3,768]{1,0:T(4,128)} %get-tuple-element.94) | copy-start | bytes 27652
  81.0 20.1 %collective-permute-start.3 = (bf16[96,2112]{1,0:T(8,128)(2,1)}, bf16[96,2112]{1,0:T(8,128)(2,1)S(1)}, u32[]{:S(2)}, u32[]{:S(2)}) collective-permute-start(bf16[96,2112]{1,0:T(8,128)(2,1)} %get-tuple-element.156), channel_id=1, source_target_pairs={{0,48},{2,14},{4,52},{6,2},{8,56},{10,6},{12,60},{14,10},{16,0},{1... | collective-permute-start | bytes 1216520 | tf_op jit(solution)/shard_map/ppermute | solution.py:76
  82.4 18.7 %collective-permute-start.2 = (bf16[96,2112]{1,0:T(8,128)(2,1)}, bf16[96,2112]{1,0:T(8,128)(2,1)S(1)}, u32[]{:S(2)}, u32[]{:S(2)}) collective-permute-start(bf16[96,2112]{1,0:T(8,128)(2,1)} %get-tuple-element.157), channel_id=1, source_target_pairs={{0,32},{2,10},{4,36},{6,14},{8,40},{10,2},{12,44},{14,6},{16,48},{... | collective-permute-start | bytes 1216520 | tf_op jit(solution)/shard_map/ppermute | solution.py:76
  82.7 18.4 %collective-permute-start.1 = (bf16[96,2112]{1,0:T(8,128)(2,1)}, bf16[96,2112]{1,0:T(8,128)(2,1)S(1)}, u32[]{:S(2)}, u32[]{:S(2)}) collective-permute-start(bf16[96,2112]{1,0:T(8,128)(2,1)} %get-tuple-element.158), channel_id=1, source_target_pairs={{0,16},{2,6},{4,20},{6,10},{8,24},{10,14},{12,28},{14,2},{16,32},{... | collective-permute-start | bytes 1216520 | tf_op jit(solution)/shard_map/ppermute | solution.py:76
  83.0 18.1 %all-to-all-start.2 = ((bf16[16,48,128]{2,1,0:T(8,128)(2,1)}), bf16[16,48,128]{2,1,0:T(8,128)(2,1)}, u32[]{:S(2)}, u32[]{:S(2)}) async-start(bf16[16,48,128]{2,1,0:T(8,128)(2,1)} %get-tuple-element.86), calls=%async_computation.2 | async-start | bytes 393216 | tf_op jit(solution)/shard_map/all_to_all | solution.py:41
  92.8 124.8 %all-gather.6.cloned.1.call-start = ((), (), s32[]{:S(2)}) async-start(), calls=%async_computation.8 | async-start | bytes 5591040 | tf_op jit(solution)/shard_map/all_gather | solution.py:774
  101.2 6.2 %copy-start.6 = (f32[2,384,64]{2,1,0:T(8,128)S(1)}, f32[2,384,64]{2,1,0:T(8,128)}, u32[]{:S(2)}) copy-start(f32[2,384,64]{2,1,0:T(8,128)} %copy-done.5) | copy-start | bytes 589828
  103.0 10.3 %collective-permute-start.6 = (bf16[4,48,896]{2,1,0:T(8,128)(2,1)S(1)}, bf16[4,48,896]{2,1,0:T(8,128)(2,1)S(1)}, u32[]{:S(2)}, u32[]{:S(2)}) collective-permute-start(bf16[4,48,896]{2,1,0:T(8,128)(2,1)S(1)} %get-tuple-element.160), channel_id=1, source_target_pairs={{0,12},{2,50},{4,0},{6,54},{8,4},{10,58},{12,8},{14,62},{16,28},{1... | collective-permute-start | bytes 1032200 | tf_op jit(solution)/shard_map/ppermute | solution.py:76
  105.4 7.9 %collective-permute-start.5 = (bf16[4,48,896]{2,1,0:T(8,128)(2,1)S(1)}, bf16[4,48,896]{2,1,0:T(8,128)(2,1)S(1)}, u32[]{:S(2)}, u32[]{:S(2)}) collective-permute-start(bf16[4,48,896]{2,1,0:T(8,128)(2,1)S(1)} %get-tuple-element.161), channel_id=1, source_target_pairs={{0,8},{2,34},{4,12},{6,38},{8,0},{10,42},{12,4},{14,46},{16,24},{1... | collective-permute-start | bytes 1032200 | tf_op jit(solution)/shard_map/ppermute | solution.py:76
  107.3 9.6 %collective-permute-start.4 = (bf16[4,48,896]{2,1,0:T(8,128)(2,1)S(1)}, bf16[4,48,896]{2,1,0:T(8,128)(2,1)S(1)}, u32[]{:S(2)}, u32[]{:S(2)}) collective-permute-start(bf16[4,48,896]{2,1,0:T(8,128)(2,1)S(1)} %get-tuple-element.162), channel_id=1, source_target_pairs={{0,4},{2,18},{4,8},{6,22},{8,12},{10,26},{12,0},{14,30},{16,20},{1... | collective-permute-start | bytes 1032200 | tf_op jit(solution)/shard_map/ppermute | solution.py:76
  117.2 4.6 %collective-permute-start.7 = (bf16[48,896]{1,0:T(8,128)(2,1)S(1)}, bf16[48,896]{1,0:T(8,128)(2,1)S(1)}, u32[]{:S(2)}, u32[]{:S(2)}) collective-permute-start(bf16[48,896]{1,0:T(8,128)(2,1)S(1)} %get-tuple-element.166), channel_id=1, source_target_pairs={{0,1},{1,64},{64,65},{65,0},{2,3},{3,66},{66,67},{67,2},{4,5},{5,6... | collective-permute-start | bytes 258056 | tf_op jit(solution)/shard_map/ppermute | solution.py:76
  117.6 4.3 %collective-permute-start.9 = (bf16[48,896]{1,0:T(8,128)(2,1)S(1)}, bf16[48,896]{1,0:T(8,128)(2,1)S(1)}, u32[]{:S(2)}, u32[]{:S(2)}) collective-permute-start(bf16[48,896]{1,0:T(8,128)(2,1)S(1)} %get-tuple-element.167), channel_id=1, source_target_pairs={{0,65},{1,0},{64,1},{65,64},{2,67},{3,2},{66,3},{67,66},{4,69},{5,... | collective-permute-start | bytes 258056 | tf_op jit(solution)/shard_map/ppermute | solution.py:76
  119.9 4.8 %collective-permute-start.8 = (bf16[48,896]{1,0:T(8,128)(2,1)S(1)}, bf16[48,896]{1,0:T(8,128)(2,1)S(1)}, u32[]{:S(2)}, u32[]{:S(2)}) collective-permute-start(bf16[48,896]{1,0:T(8,128)(2,1)S(1)} %get-tuple-element.168), channel_id=1, source_target_pairs={{0,64},{1,65},{64,0},{65,1},{2,66},{3,67},{66,2},{67,3},{4,68},{5,... | collective-permute-start | bytes 258056 | tf_op jit(solution)/shard_map/ppermute | solution.py:76
  144.3 5.2 %copy-start.12 = (bf16[48,3072]{1,0:T(8,128)(2,1)S(1)}, bf16[48,3072]{1,0:T(8,128)(2,1)}, u32[]{:S(2)}) copy-start(bf16[48,3072]{1,0:T(8,128)(2,1)} %get-tuple-element.108) | copy-start | bytes 884740
  144.3 5.2 %copy-start.13 = (f32[48,768]{1,0:T(8,128)S(1)}, f32[48,768]{1,0:T(8,128)}, u32[]{:S(2)}) copy-start(f32[48,768]{1,0:T(8,128)} %get-tuple-element.107) | copy-start | bytes 442372
  145.6 13.8 %all-to-all-start.4 = ((bf16[32,32,192]{2,1,0:T(8,128)(2,1)}), bf16[32,32,192]{2,1,0:T(8,128)(2,1)S(1)}, u32[]{:S(2)}, u32[]{:S(2)}) async-start(bf16[32,32,192]{2,1,0:T(8,128)(2,1)} %pad_maximum_fusion), calls=%async_computation.4 | async-start | bytes 1048576 | tf_op jit(solution)/shard_map/all_to_all | solution.py:41
  149.5 3.3 %copy-start.7 = (bf16[1,256,768]{2,1,0:T(8,128)(2,1)S(1)}, bf16[1,256,768]{2,1,0:T(8,128)(2,1)}, u32[]{:S(2)}) copy-start(bf16[1,256,768]{2,1,0:T(8,128)(2,1)} %param.16) | copy-start | bytes 1179652
  173.3 32.0 %collective-permute-start.12 = (bf16[16,24,640]{2,1,0:T(8,128)(2,1)S(1)}, bf16[16,24,640]{2,1,0:T(8,128)(2,1)S(1)}, u32[]{:S(2)}, u32[]{:S(2)}) collective-permute-start(bf16[16,24,640]{2,1,0:T(8,128)(2,1)S(1)} %all_to_all.36.refs_1_), channel_id=1, source_target_pairs={{48,0},{0,16},{16,32},{32,48},{49,1},{1,17},{17,33},{33,49},{50,2}... | collective-permute-start | bytes 1474568 | tf_op jit(solution)/shard_map/ppermute | solution.py:804
  173.8 31.5 %collective-permute-start.11 = (bf16[16,24,640]{2,1,0:T(8,128)(2,1)S(1)}, bf16[16,24,640]{2,1,0:T(8,128)(2,1)S(1)}, u32[]{:S(2)}, u32[]{:S(2)}) collective-permute-start(bf16[16,24,640]{2,1,0:T(8,128)(2,1)S(1)} %all_to_all.36.refs_1_), channel_id=1, source_target_pairs={{32,0},{48,16},{0,32},{16,48},{33,1},{49,17},{1,33},{17,49},{34,2}... | collective-permute-start | bytes 1474568 | tf_op jit(solution)/shard_map/ppermute | solution.py:804
  175.6 32.4 %collective-permute-start.10 = (bf16[16,24,640]{2,1,0:T(8,128)(2,1)S(1)}, bf16[16,24,640]{2,1,0:T(8,128)(2,1)S(1)}, u32[]{:S(2)}, u32[]{:S(2)}) collective-permute-start(bf16[16,24,640]{2,1,0:T(8,128)(2,1)S(1)} %all_to_all.36.refs_1_), channel_id=1, source_target_pairs={{16,0},{32,16},{48,32},{0,48},{17,1},{33,17},{49,33},{1,49},{18,2}... | collective-permute-start | bytes 1474568 | tf_op jit(solution)/shard_map/ppermute | solution.py:804
  208.0 7.5 %collective-permute-start.13 = (bf16[16,24,640]{2,1,0:T(8,128)(2,1)S(1)}, bf16[16,24,640]{2,1,0:T(8,128)(2,1)S(1)}, u32[]{:S(2)}, u32[]{:S(2)}) collective-permute-start(bf16[16,24,640]{2,1,0:T(8,128)(2,1)S(1)} %all_to_all.36.refs_1_), channel_id=1, source_target_pairs={{0,2},{2,0},{1,3},{3,1},{4,6},{6,4},{5,7},{7,5},{8,10},{10,8},{9,1... | collective-permute-start | bytes 1474568 | tf_op jit(solution)/shard_map/ppermute | solution.py:103
  214.0 2.2 collective-permute-start.14
  214.0 0.8 copy-start.1
  214.8 2.1 collective-permute-start.15
  215.3 2.3 collective-permute-start.16
  217.6 11.9 %collective-permute-start.17 = (bf16[64,48,896]{2,1,0:T(8,128)(2,1)}, bf16[64,48,896]{2,1,0:T(8,128)(2,1)S(1)}, u32[]{:S(2)}, u32[]{:S(2)}) collective-permute-start(bf16[64,48,896]{2,1,0:T(8,128)(2,1)} %bitcast.76), channel_id=1, source_target_pairs={{0,2},{2,0},{1,3},{3,1},{4,6},{6,4},{5,7},{7,5},{8,10},{10,8},{9,1... | collective-permute-start | bytes 16515080 | tf_op jit(solution)/shard_map/ppermute | solution.py:103
  218.1 2.6 %copy-start = (bf16[3072,896]{1,0:T(8,128)(2,1)S(1)}, bf16[3072,896]{1,0:T(8,128)(2,1)}, u32[]{:S(2)}) copy-start(bf16[3072,896]{1,0:T(8,128)(2,1)} %all-gather.6.cloned.1.call-done) | copy-start | bytes 16515076
  220.6 1.0 copy-start.2
  229.4 8.1 %copy-start.3 = (f32[768,64]{1,0:T(8,128)}, f32[768,64]{1,0:T(8,128)S(1)}, u32[]{:S(2)}) copy-start(f32[768,64]{1,0:T(8,128)S(1)} %get-tuple-element.139) | copy-start | bytes 589828
  237.4 2.1 copy-start.14
  237.5 2.1 copy-start.15
  237.5 1.0 copy-start.4
  238.9 1.2 copy-start.16
Sparse Core Ops, SparseCore 0:
  29.1 48.5 all-gather.3
  125.6 88.2 all-gather.5
where the time goes:
time: 248 us; the launch traced here: 247 us
  blocking collectives  52 us (21%)
  starting transfers between devices  50.4 us (20%)
  waiting for transfers between devices  49.1 us (20%)
  Pallas kernels  46.6 us (19%)
  local copies, waits for them, and re-layouts  17.7 us (7%)
  between operations  15.2 us (6%)
  matrix products  11.8 us (5%)
  other arithmetic  4.14 us (2%)
    all_to_all x3, blocking collectives, swap(): return lax.all_to_all(parts, axes, split_axis=0, concat_axis=0, tiled=True)  52 us
    all_to_all x4, waiting for transfers between devices, swap(): return lax.all_to_all(parts, axes, split_axis=0, concat_axis=0, tiled=True)  33.9 us
    all_to_all x4, starting transfers between devices, swap(): return lax.all_to_all(parts, axes, split_axis=0, concat_axis=0, tiled=True)  29.8 us
    pallas_call x2, Pallas kernels, place(): pl.pallas_call(functools.partial(place_kernel, 1 if before else 0), out_s...  15.6 us
    dot_general x5, matrix products, dot(): lax.dot_general(left, right, (dims, ((), ())), precision=precision, prefe...  11.8 us
    ppermute x9, starting transfers between devices, ring_swap(): mine.append(lax.ppermute(part, axes, pairs_of(step)))  9.13 us
    ppermute x9, waiting for transfers between devices, ring_swap(): mine.append(lax.ppermute(part, axes, pairs_of(step)))  8.57 us
    pallas_call x1, Pallas kernels, feed(): pl.pallas_call(feed_kernel, out_shape=(jax.ShapeDtypeStruct((4, SLOTS, 2...  8.28 us
  transfers between devices with their start and end apart: 24, of which 14 were waited for; matrix products, arithmetic and copies ran while one was open for 10% of the time, Pallas kernels for 13%

commit v1 on v0

--- a/solution.py
+++ b/solution.py
@@ -1,9 +1,7 @@
 import functools
-import itertools
 
 import jax
 import jax.numpy as jnp
-import numpy as np
 from jax import lax
 from jax.experimental import pallas as pl
 from jax.experimental.pallas import tpu as pltpu
@@ -77,42 +75,8 @@
     return mine
 
 
-EVERY = ("yh", "x", "z", "c", "yl")
-UNIT_ORDERS = (("x", "y", "z"), ("z", "x", "y"))
-
-
-def gather_pairs(orders, stage, step):
-    pairs = []
-    for place in itertools.product(range(2), range(4), range(4), range(2), range(2)):
-        yh, x, z, c, yl = place
-        at = {"x": x, "y": yh * 2 + yl, "z": z}
-        axis = orders[c][stage]
-        at[axis] = (at[axis] + step) % 4
-        source = (at["y"] // 2, at["x"], at["z"], c, at["y"] % 2)
-        pairs.append(tuple(int(np.ravel_multi_index(p, (2, 4, 4, 2, 2))) for p in (source, place)))
-    return pairs
-
-
-def gather_step(part, orders, stage):
-    return [part] + [
-        lax.ppermute(part, EVERY, gather_pairs(orders, stage, step)) for step in (1, 2, 3)
-    ]
-
-
 def other_core(pieces):
     return [lax.ppermute(piece, "c", [(0, 1), (1, 0)]) for piece in pieces]
-
-
-def chip_at(orders, core, me_ref, steps):
-    at = {
-        axis: (me_ref["xyz".index(axis)] + step) & 3
-        for axis, step in zip(orders[core], steps, strict=True)
-    }
-    return at["x"], at["y"], at["z"]
-
-
-def steps_to(orders, core, me_ref, chip):
-    return [(chip["xyz".index(axis)] - me_ref["xyz".index(axis)]) & 3 for axis in orders[core]]
 
 
 def dot(left, right, dims, precision=None):
@@ -148,124 +112,128 @@
     return inv * (scaled - mean_one - unit * mean_two)
 
 
-def place_kernel(other, me_ref, *refs):
-    units_in, pieces, refs = refs[0], refs[1:5], refs[5:]
+def place_kernel(
+    other, me_ref, units_in, *refs
+):
     if other:
-        refs = refs[6:]
+        refs = refs[3:]
     (
-        expand_ref, contract_ref, out_ref, key_ref, value_ref, query_ref, sums_ref, vector_ref,
-        land_ref, land_heads_ref, stage_ref, tiles_ref, heads_ref, in_sems, out_sems,
+        expand_ref, contract_ref, out_ref, vector_ref,
+        land_ref, stage_ref, tiles_ref, in_sems, out_sems,
     ) = refs
 
-    def take(i):
-        if i < 4:
-            rows = pl.ds(i * 16, 16)
-            return pltpu.make_async_copy(units_in.at[rows], land_ref.at[rows], in_sems.at[i])
-        return pltpu.make_async_copy(pieces[i - 4], land_heads_ref.at[i - 4], in_sems.at[i])
-
-    for i in range(8):
-        take(i).start()
+    def take(x):
+        rows = pl.ds(x * 16, 16)
+        return pltpu.make_async_copy(units_in.at[rows], land_ref.at[rows], in_sems.at[x])
+
+    for x in range(4):
+        take(x).start()
 
     def emit(core):
         for x in range(4):
             take(x).wait()
             for y in range(4):
                 for z in range(4):
-                    at = x * 16 + y * 4 + z
                     staged = stage_ref.at[x, y * 4 + z]
-                    staged[...] = land_ref[at, :, :D].astype(F32)
+                    staged[...] = land_ref[x * 16 + y * 4 + z, :, :D].astype(F32)
                     if core == 0:
-                        row = (z * 4 + y) * 48
-                        cols = pl.ds(x * D, D)
-                        target = expand_ref.at[pl.ds(row, 48), cols]
+                        target = expand_ref.at[pl.ds((z * 4 + y) * 48, 48), pl.ds(x * D, D)]
                     else:
-                        row = z * D + (x * 4 + y) * 48
-                        target = contract_ref.at[pl.ds(row, 48), :]
+                        target = contract_ref.at[pl.ds(z * D + (x * 4 + y) * 48, 48), :]
                     pltpu.make_async_copy(staged, target, out_sems.at[x]).start()
 
-        def unit_shard(unit, at16, cols):
+        def unit_shard(unit, at16):
             if core == 0:
-                chip = (unit, at16 % 4, at16 // 4)
+                x, y, z = unit, at16 % 4, at16 // 4
             else:
-                chip = (at16 // 4, at16 % 4, unit)
-            x, y, z = chip
-            return land_ref[x * 16 + y * 4 + z, :, cols].astype(F32)
+                x, y, z = at16 // 4, at16 % 4, unit
+            return land_ref[x * 16 + y * 4 + z, :, D:].astype(F32)
 
         for row in range(8):
             tiles_ref[row * 48 : (row + 1) * 48, :] = jnp.concatenate(
                 [
-                    unit_shard(unit, row * 2 + half, slice(D, 896))[:, :96]
+                    unit_shard(unit, row * 2 + half)[:, :96]
                     for unit in range(4)
                     for half in range(2)
                 ],
                 axis=1,
             )
-        rows = pl.ds(core * 384, 384)
-        copies = [pltpu.make_async_copy(tiles_ref, out_ref.at[rows, :], out_sems.at[4])]
-        copies[0].start()
+        copy = pltpu.make_async_copy(
+            tiles_ref, out_ref.at[pl.ds(core * 384, 384), :], out_sems.at[4]
+        )
+        copy.start()
         for at16 in range(16):
-            vector_ref[at16] = sum(unit_shard(unit, at16, slice(D, 896)) for unit in range(4))
-        for i in range(4, 8):
-            take(i).wait()
+            vector_ref[at16] = sum(unit_shard(unit, at16)[:, 96:] for unit in range(4))
         for x in range(4):
-            for z in range(4):
-                for yl in range(2):
-                    halves = [
-                        land_heads_ref[(x - me_ref[0]) & 3, (yh * 2 + yl) * 4 + z].astype(F32)
-                        for yh in range(2)
-                    ]
-                    at = slice(((x * 4 + z) * 2 + yl) * 24, ((x * 4 + z) * 2 + yl + 1) * 24)
-                    for kind in range(3):
-                        cols = slice(kind * 192, (kind + 1) * 192)
-                        heads_ref[kind, at, :] = jnp.concatenate(
-                            [half[:, cols] for half in halves], axis=1
-                        )
-                    sums_ref[at, :] = halves[0][:, 576:] + halves[1][:, 576:]
-        cols = pl.ds(core * 384, 384)
-        for kind, target in enumerate((key_ref, value_ref, query_ref)):
-            copies.append(
-                pltpu.make_async_copy(
-                    heads_ref.at[kind], target.at[:, cols], out_sems.at[5 + kind]
-                )
-            )
-            copies[-1].start()
-        for k3 in range(4):
-            held = stage_ref.at[k3]
-            pltpu.make_async_copy(held, held, out_sems.at[k3]).wait()
-        for copy in copies:
-            copy.wait()
+            held = stage_ref.at[x]
+            pltpu.make_async_copy(held, held, out_sems.at[x]).wait()
+        copy.wait()
 
     for core in range(2):
         pl.when((me_ref[3] + other & 1) == core)(functools.partial(emit, core))
 
 
-def place(me, pieces, before=None):
-    before = () if before is None else tuple(before[:6])
+def place(me, units, before=None):
+    before = () if before is None else tuple(before[:3])
     return pl.pallas_call(
         functools.partial(place_kernel, 1 if before else 0),
         out_shape=(
             jax.ShapeDtypeStruct((D, FF), F32),
             jax.ShapeDtypeStruct((FF, D), F32),
-        )
-        + (jax.ShapeDtypeStruct((D, D), F32),) * 4
-        + (jax.ShapeDtypeStruct((D, HEAD), F32), jax.ShapeDtypeStruct((16, 48, 128), F32)),
-        in_specs=[SMEM_SPEC]
-        + [ANY_SPEC] * 5
-        + [ANY_SPEC] * len(before),
-        out_specs=(ANY_SPEC,) * 6 + (VMEM_SPEC,) * 2,
+            jax.ShapeDtypeStruct((D, D), F32),
+            jax.ShapeDtypeStruct((16, 48, 32), F32),
+        ),
+        in_specs=[SMEM_SPEC, ANY_SPEC] + [ANY_SPEC] * len(before),
+        out_specs=(ANY_SPEC,) * 3 + (VMEM_SPEC,),
         scratch_shapes=[
             pltpu.VMEM((64, 48, 896), BF16),
-            pltpu.VMEM((4, 16, 24, 640), BF16),
             pltpu.VMEM((4, 16, 48, D), F32),
             pltpu.VMEM((384, D), F32),
-            pltpu.VMEM((3, D, 384), F32),
-            pltpu.SemaphoreType.DMA((8,)),
-            pltpu.SemaphoreType.DMA((8,)),
+            pltpu.SemaphoreType.DMA((4,)),
+            pltpu.SemaphoreType.DMA((5,)),
         ],
-        input_output_aliases={6 + i: i for i in range(6)} if before else {},
-        compiler_params=pltpu.CompilerParams(vmem_limit_bytes=40 * 2**20),
+        input_output_aliases={2 + i: i for i in range(3)} if before else {},
+        compiler_params=pltpu.CompilerParams(vmem_limit_bytes=32 * 2**20),
         cost_estimate=pl.CostEstimate(flops=0, bytes_accessed=20 * 2**20, transcendentals=0),
-    )(me, *pieces, *before)
+    )(me, units, *before)
+
+
+def place_heads_kernel(me_ref, own_ref, other_ref, key_ref, value_ref, query_ref, sums_ref):
+    def emit(by_core):
+        for x in range(4):
+            for z in range(4):
+                for yl in range(2):
+                    blocks = [
+                        by_core[c][x * 16 + (yh * 2 + yl) * 4 + z].astype(F32)
+                        for c in range(2)
+                        for yh in range(2)
+                    ]
+                    at = ((x * 4 + z) * 2 + yl) * 24
+                    for kind, out_ref in enumerate((key_ref, value_ref, query_ref)):
+                        out_ref[at : at + 24, :] = jnp.concatenate(
+                            [block[:, kind * 192 : (kind + 1) * 192] for block in blocks], axis=1
+                        )
+                    sums_ref[at : at + 24, :] = sum(block[:, 576:] for block in blocks)
+
+    @pl.when(me_ref[3] == 0)
+    def _():
+        emit((own_ref, other_ref))
+
+    @pl.when(me_ref[3] == 1)
+    def _():
+        emit((other_ref, own_ref))
+
+
+def place_heads(me, own, other):
+    return pl.pallas_call(
+        place_heads_kernel,
+        out_shape=(jax.ShapeDtypeStruct((D, D), F32),) * 3
+        + (jax.ShapeDtypeStruct((D, HEAD), F32),),
+        in_specs=[SMEM_SPEC] + [VMEM_SPEC] * 2,
+        out_specs=(VMEM_SPEC,) * 4,
+        compiler_params=pltpu.CompilerParams(vmem_limit_bytes=18 * 2**20),
+        cost_estimate=pl.CostEstimate(flops=0, bytes_accessed=12 * 2**20, transcendentals=0),
+    )(me, own, other)
 
 
 def embed_kernel(
@@ -798,14 +766,22 @@
     )
     own_qkv = jnp.concatenate([grad_qkv, jnp.pad(norm_sums, ((0, 0), (0, 62)))], axis=1)
     own_qkv = own_qkv.astype(BF16)
-    heads = spread(own_qkv, ("yh", "yl", "z"))
+    heads = spread(own_qkv, CHIPS)
     heads, grad_heads = lax.optimization_barrier((heads, grad_heads))
-    heads = [heads] + [
-        lax.ppermute(heads, "x", [((i + step) % 4, i) for i in range(4)]) for step in (1, 2, 3)
-    ]
     back = swap(
         jnp.pad(grad_heads, ((0, 0), (0, HEAD))).reshape(16, SLOTS, 4 * HEAD), SIXTEEN
     )
+    heads_other = lax.ppermute(heads, "c", [(0, 1), (1, 0)])
+    me = jnp.stack([x_at, y_at, z_at, core_at])
+    final_key, final_value, final_query, norm_sums = place_heads(me, heads, heads_other)
+    norm_sums = norm_sums[:, :2].T
+    grad_gain_one = (norm_sums[0] - bias_one * norm_sums[1]) / gain_one
+    grad_bias_one = norm_sums[1]
+    units, back, final_key, grad_gain_one = lax.optimization_barrier(
+        (units, back, final_key, grad_gain_one)
+    )
+    first = place(me, units)
+    back, first = lax.optimization_barrier((back, first))
     input_grad = embed_back(
         back,
         routed_x,
@@ -819,17 +795,9 @@
         w_value,
         w_query,
     )
-    heads, input_grad = lax.optimization_barrier((heads, input_grad))
-    heads = heads + other_core(heads)
-    units, heads = lax.optimization_barrier((units, heads))
-    me = jnp.stack([x_at, y_at, z_at, core_at])
-    first = place(me, [units] + heads[:4])
-    placed = place(me, other_core([units]) + heads[4:], first)
-    final_expand, final_contract, final_out, final_key, final_value, final_query = placed[:6]
-    norm_sums = (first[6][:, :2] + placed[6][:, :2]).T
-    grad_gain_one = (norm_sums[0] - bias_one * norm_sums[1]) / gain_one
-    grad_bias_one = norm_sums[1]
-    vectors = first[7][:, :, 96:] + placed[7][:, :, 96:]
+    placed = place(me, other_core([units])[0], first)
+    final_expand, final_contract, final_out = placed[:3]
+    vectors = first[3] + placed[3]
     vectors = vectors[:, :, :3].reshape(3, D)
     return (
         output[None],

time: 248 us -> 243 us (0.980)
  blocking collectives: 52 us -> 46.7 us
    all_to_all x4 -> x5, waiting for transfers between devices: 33.9 us -> 40.9 us  [swap(): return lax.all_to_all(parts, axes, split_axis=0, concat_axis=0, tiled=True)]
    ppermute x5 -> x1, starting transfers between devices: 6.93 us -> 0.71 us  [other_core(): return [lax.ppermute(piece, 'c', [(0, 1), (1, 0)]) for piece in pieces]]
    pallas_call x0 -> x1, Pallas kernels: none -> 5.66 us  [place_heads(): pl.pallas_call(place_heads_kernel, out_shape=(jax.ShapeDtypeStruct((D, D)...]
    all_to_all x3 -> x2, blocking collectives: 52 us -> 46.7 us  [swap(): return lax.all_to_all(parts, axes, split_axis=0, concat_axis=0, tiled=True)]
    pallas_call x2, Pallas kernels: 15.6 us -> 10.6 us  [place(): pl.pallas_call(functools.partial(place_kernel, 1 if before else 0), out_s...]
    all_to_all x4 -> x5, starting transfers between devices: 29.8 us -> 33.2 us  [swap(): return lax.all_to_all(parts, axes, split_axis=0, concat_axis=0, tiled=True)]
    ppermute x3 -> x1, waiting for transfers between devices: 2.65 us -> 0.01 us  [body(): heads_other = lax.ppermute(heads, 'c', [(0, 1), (1, 0)])]
    ppermute x3 -> x1, starting transfers between devices: 3.54 us -> 5.22 us  [body(): heads_other = lax.ppermute(heads, 'c', [(0, 1), (1, 0)])]
  transfers between devices with their start and end apart: 24 -> 19, of which waited for: 14 -> 10; matrix products, arithmetic and copies ran while one was open for 10% -> 10% of each run, Pallas kernels for 13% -> 15%
where the time goes in v1:
time: 243 us; the launch traced here: 242 us
  waiting for transfers between devices  51.2 us (21%)
  starting transfers between devices  49.3 us (20%)
  Pallas kernels  47.3 us (19%)
  blocking collectives  46.7 us (19%)
  local copies, waits for them, and re-layouts  16.6 us (7%)
  between operations  15.2 us (6%)
  matrix products  11.9 us (5%)
  other arithmetic  4.11 us (2%)
    all_to_all x2, blocking collectives, swap(): return lax.all_to_all(parts, axes, split_axis=0, concat_axis=0, tiled=True)  46.7 us
    all_to_all x5, waiting for transfers between devices, swap(): return lax.all_to_all(parts, axes, split_axis=0, concat_axis=0, tiled=True)  40.9 us
    all_to_all x5, starting transfers between devices, swap(): return lax.all_to_all(parts, axes, split_axis=0, concat_axis=0, tiled=True)  33.2 us
    dot_general x5, matrix products, dot(): lax.dot_general(left, right, (dims, ((), ())), precision=precision, prefe...  11.9 us
    pallas_call x2, Pallas kernels, place(): pl.pallas_call(functools.partial(place_kernel, 1 if before else 0), out_s...  10.6 us
    ppermute x9, starting transfers between devices, ring_swap(): mine.append(lax.ppermute(part, axes, pairs_of(step)))  9.13 us
    ppermute x9, waiting for transfers between devices, ring_swap(): mine.append(lax.ppermute(part, axes, pairs_of(step)))  8.57 us
    pallas_call x1, Pallas kernels, feed(): pl.pallas_call(feed_kernel, out_shape=(jax.ShapeDtypeStruct((4, SLOTS, 2...  8.28 us
  transfers between devices with their start and end apart: 19, of which 10 were waited for; matrix products, arithmetic and copies ran while one was open for 10% of the time, Pallas kernels for 15%

profile of v1, /device:TPU:1, one launch (start us, length us, event | category | flops | bytes accessed | tf_op | source)
XLA Modules:
  0.0 242.3 jit_solution(2854308498490995031)
XLA Ops:
  8.4 4.7 %shard_map.255 = (bf16[4,16,48,256]{3,2,1,0:T(8,128)(2,1)}, bf16[48,768]{1,0:T(8,128)(2,1)}, f32[48,768]{1,0:T(8,128)}) custom-call(s32[2]{0:T(128)} %pad_add_fusion.count_ref, s32[1,48]{1,0:T(1,128)} %bitcast.91, s32[1,256]{1,0:T(1,128)} %ids_ref.1, bf16[256,768]{1,0:T(8,128)(2,1)} %bitcast.84, f32[768]{0:T(1024)} %gain_ref.3, f32[768]{0:T(1024)} %bias_ref.1, ...), custom_call_target="tpu_custom_call" | custom-call | flops 169869312 | bytes 6291456 | tf_op jit(solution)/shard_map/pallas_call | solution.py:287
  13.1 12.6 %all-to-all-start = ((bf16[64,48,256]{2,1,0:T(8,128)(2,1)}), bf16[64,48,256]{2,1,0:T(8,128)(2,1)S(1)}, u32[]{:S(2)}, u32[]{:S(2)}) async-start(bf16[64,48,256]{2,1,0:T(8,128)(2,1)} %bitcast.83), calls=%async_computation | async-start | bytes 3145728 | tf_op jit(solution)/shard_map/all_to_all | solution.py:39
  26.5 0.8 dynamic_slice.50
  27.3 0.8 dynamic_slice.48
  28.1 0.8 dynamic_slice.49
  29.2 0.9 fusion.11
  30.1 20.7 %all-to-all-done = bf16[64,48,256]{2,1,0:T(8,128)(2,1)S(1)} async-done(((bf16[64,48,256]{2,1,0:T(8,128)(2,1)}), bf16[64,48,256]{2,1,0:T(8,128)(2,1)S(1)}, u32[]{:S(2)}, u32[]{:S(2)}) %all-to-all-start) | async-done | bytes 1572896 | tf_op jit(solution)/shard_map/all_to_all | solution.py:39
  50.8 4.5 %shard_map.256 = (f32[2,384,64]{2,1,0:T(8,128)S(1)}, bf16[2,384,128]{2,1,0:T(8,128)(2,1)}, f32[2,1,384]{2,1,0:T(1,128)S(1)}) custom-call(s32[1]{0:T(128)} %bitcast.x_ref, bf16[4,2,384,256]{3,2,1,0:T(8,128)(2,1)S(1)} %bitcast.78), custom_call_target="tpu_custom_call" | custom-call | flops 3623878656 | bytes 3145728 | tf_op jit(solution)/shard_map/pallas_call | solution.py:362
  55.3 0.7 copy-done.1
  56.0 3.5 %all-to-all-start.1 = ((bf16[16,48,128]{2,1,0:T(8,128)(2,1)}), bf16[16,48,128]{2,1,0:T(8,128)(2,1)S(1)}, u32[]{:S(2)}, u32[]{:S(2)}) async-start(bf16[16,48,128]{2,1,0:T(8,128)(2,1)} %bitcast.7), calls=%async_computation.1 | async-start | bytes 393216 | tf_op jit(solution)/shard_map/all_to_all | solution.py:39
  59.6 4.6 %fusion.12.grad_act_ref = f32[48,3072]{1,0:T(8,128)} fusion(bf16[48,768]{1,0:T(8,128)(2,1)S(1)} %get-tuple-element.154.low_ref, bf16[3072,768]{1,0:T(8,128)(2,1)} %param.27), kind=kOutput, calls=%fused_computation.61 | convolution fusion | flops 226492416 | bytes 5382144 | tf_op jit(solution)/shard_map/dot_general | solution.py:83
  66.1 1.7 all-to-all-done.1.parts_ref
  68.4 8.3 %shard_map.257 = (bf16[4,48,2112]{2,1,0:T(8,128)(2,1)}, bf16[4,48,2112]{2,1,0:T(8,128)(2,1)}, bf16[16,48,128]{2,1,0:T(8,128)(2,1)}, f32[48,768]{1,0:T(8,128)}, f...) custom-call(bf16[16,48,128]{2,1,0:T(8,128)(2,1)} %copy-done.7, ...), custom_call_target="tpu_custom_call" | custom-call | flops 566231040 | bytes 10485760 | tf_op jit(solution)/shard_map/pallas_call | solution.py:523
  76.7 0.9 collective-permute-start
  77.7 1.2 constant_dynamic-update-slice_fusion.1
  78.9 1.0 collective-permute-done
  80.0 1.1 dynamic-slice_bitcast_fusion
  81.0 1.4 collective-permute-start.3
  83.0 9.8 %all-to-all-start.2 = ((bf16[16,48,128]{2,1,0:T(8,128)(2,1)}), bf16[16,48,128]{2,1,0:T(8,128)(2,1)}, u32[]{:S(2)}, u32[]{:S(2)}) async-start(bf16[16,48,128]{2,1,0:T(8,128)(2,1)} %get-tuple-element.77), calls=%async_computation.2 | async-start | bytes 393216 | tf_op jit(solution)/shard_map/all_to_all | solution.py:39
  92.9 1.0 reshape.120
  93.9 1.0 pad.13.refs_4_
  94.9 6.2 %all-to-all-done.2 = bf16[16,48,128]{2,1,0:T(8,128)(2,1)} async-done(((bf16[16,48,128]{2,1,0:T(8,128)(2,1)}), bf16[16,48,128]{2,1,0:T(8,128)(2,1)}, u32[]{:S(2)}, u32[]{:S(2)}) %all-to-all-start.2) | async-done | bytes 196640 | tf_op jit(solution)/shard_map/all_to_all | solution.py:39
  101.2 1.6 shard_map.258
  103.0 2.4 %collective-permute-start.6 = (bf16[4,48,896]{2,1,0:T(8,128)(2,1)S(1)}, bf16[4,48,896]{2,1,0:T(8,128)(2,1)S(1)}, u32[]{:S(2)}, u32[]{:S(2)}) collective-permute-start(bf16[4,48,896]{2,1,0:T(8,128)(2,1)S(1)} %get-tuple-element.142), channel_id=1, source_target_pairs={{0,12},{2,50},{4,0},{6,54},{8,4},{10,58},{12,8},{14,62},{16,28},{1... | collective-permute-start | bytes 1032200 | tf_op jit(solution)/shard_map/ppermute | solution.py:74
  105.4 2.0 collective-permute-start.5
  107.4 5.9 %shard_map.259 = (bf16[2,384,64]{2,1,0:T(8,128)(2,1)S(1)}, bf16[4,2,384,128]{3,2,1,0:T(8,128)(2,1)S(1)}) custom-call(s32[1]{0:T(128)} %bitcast.x_ref, bf16[4,2,384,256]{3,2,1,0:T(8,128)(2,1)S(1)} %bitcast.79, bf16[2,384,128]{2,1,0:T(8,128)(2,1)} %bitcast.21.do_ref, f32[2,384,64]{2,1,0:T(8,128)S(1)} %copy-done.2, f32[2,1,384]{2,1,0:T(1,128)S(1)} %get-tuple-element.89.lse_ref), custom_call_target="tpu_custom_call" | custom-call | flops 9059696640 | bytes 6291456 | tf_op jit(solution)/shard_map/pallas_call | solution.py:422
  113.3 3.6 %collective-permute-done.4 = bf16[4,48,896]{2,1,0:T(8,128)(2,1)S(1)} collective-permute-done((bf16[4,48,896]{2,1,0:T(8,128)(2,1)S(1)}, bf16[4,48,896]{2,1,0:T(8,128)(2,1)S(1)}, u32[]{:S(2)}, u32[]{:S(2)}) %collective-permute-start.4) | collective-permute-done | bytes 344096 | tf_op jit(solution)/shard_map/ppermute | solution.py:74
  117.6 2.4 collective-permute-start.9
  120.0 1.9 collective-permute-done.7
  121.9 2.9 %collective-permute-done.8 = bf16[48,896]{1,0:T(8,128)(2,1)S(1)} collective-permute-done((bf16[48,896]{1,0:T(8,128)(2,1)S(1)}, bf16[48,896]{1,0:T(8,128)(2,1)S(1)}, u32[]{:S(2)}, u32[]{:S(2)}) %collective-permute-start.8) | collective-permute-done | bytes 86048 | tf_op jit(solution)/shard_map/ppermute | solution.py:74
  125.5 16.9 %all_to_all.35 = bf16[4,2,384,128]{3,2,1,0:T(8,128)(2,1)S(1)} all-to-all(bf16[4,2,384,128]{3,2,1,0:T(8,128)(2,1)S(1)} %get-tuple-element.96), channel_id=1, replica_groups=mesh['yh'=2,'x'=4,'z'=4,'c'=2,'yl'=2] {'x'}, dimensions={0} | all-to-all | bytes 1572864 | tf_op jit(solution)/shard_map/all_to_all | solution.py:39
  142.6 1.7 convolution_convert_fusion
  144.7 0.9 pad_maximum_fusion
  145.6 3.9 %all-to-all-start.4 = ((bf16[32,32,192]{2,1,0:T(8,128)(2,1)}), bf16[32,32,192]{2,1,0:T(8,128)(2,1)S(1)}, u32[]{:S(2)}, u32[]{:S(2)}) async-start(bf16[32,32,192]{2,1,0:T(8,128)(2,1)} %pad_maximum_fusion), calls=%async_computation.4 | async-start | bytes 1048576 | tf_op jit(solution)/shard_map/all_to_all | solution.py:39
  149.6 3.3 %fusion.1 = f32[48,768]{1,0:T(8,128)S(1)} fusion(f32[48,768]{1,0:T(8,128)S(1)} %copy-done.10, bf16[48,3072]{1,0:T(8,128)(2,1)S(1)} %copy-done.9, bf16[3072,768]{1,0:T(8,128)(2,1)} %param.27, f32[48]{0:T(128)S(1)} %get-tuple-element.136), kind=kOutput, calls=%fused_computation.4 | convolution fusion | flops 226566144 | bytes 5308608 | tf_op jit(solution)/shard_map/dot_general | solution.py:83
  152.8 1.3 fusion
  154.2 5.2 %all-to-all-done.4 = bf16[32,32,192]{2,1,0:T(8,128)(2,1)S(1)} async-done(((bf16[32,32,192]{2,1,0:T(8,128)(2,1)}), bf16[32,32,192]{2,1,0:T(8,128)(2,1)S(1)}, u32[]{:S(2)}, u32[]{:S(2)}) %all-to-all-start.4) | async-done | bytes 393248 | tf_op jit(solution)/shard_map/all_to_all | solution.py:39
  160.6 29.8 %all_to_all.36.own_ref = bf16[64,24,640]{2,1,0:T(8,128)(2,1)S(1)} all-to-all(bf16[64,24,640]{2,1,0:T(8,128)(2,1)S(1)} %broadcast_in_dim.47), channel_id=1, replica_groups=mesh['yh'=2,'x'=4,'z'=4,'c'=2,'yl'=2] {'x','yh','yl','z'}, dimensions={0} | all-to-all | bytes 3932160 | tf_op jit(solution)/shard_map/all_to_all | solution.py:39
  190.4 5.2 %collective-permute-start.10 = (bf16[64,24,640]{2,1,0:T(8,128)(2,1)S(1)}, bf16[64,24,640]{2,1,0:T(8,128)(2,1)}, u32[]{:S(2)}, u32[]{:S(2)}) collective-permute-start(bf16[64,24,640]{2,1,0:T(8,128)(2,1)S(1)} %all_to_all.36.own_ref), channel_id=1, source_target_pairs={{0,2},{2,0},{1,3},{3,1},{4,6},{6,4},{5,7},{7,5},{8,10},{10,8},{9,1... | collective-permute-start | bytes 5898248 | tf_op jit(solution)/shard_map/ppermute | solution.py:774
  195.7 0.8 pad.15
  196.5 3.5 %all-to-all-start.6 = ((bf16[16,48,256]{2,1,0:T(8,128)(2,1)}), bf16[16,48,256]{2,1,0:T(8,128)(2,1)S(1)}, u32[]{:S(2)}, u32[]{:S(2)}) async-start(bf16[16,48,256]{2,1,0:T(8,128)(2,1)} %bitcast.37), calls=%async_computation.6 | async-start | bytes 786432 | tf_op jit(solution)/shard_map/all_to_all | solution.py:39
  200.0 5.7 %shard_map.260 = (f32[768,768]{1,0:T(8,128)}, f32[768,768]{1,0:T(8,128)}, f32[768,768]{1,0:T(8,128)}, f32[768,64]{1,0:T(8,128)S(1)}) custom-call(s32[4]{0:T(128)S(1)} %pad_add_fusion.1.me_ref, bf16[64,24,640]{2,1,0:T(8,128)(2,1)S(1)} %all_to_all.36.own_ref, bf16[64,24,640]{2,1,0:T(8,128)(2,1)} %collective-permute-done.10.other_ref), custom_call_target="tpu_custom_call" | custom-call | bytes 12582912 | tf_op jit(solution)/shard_map/pallas_call | solution.py:228
  206.7 7.1 %all-to-all-done.6.back_ref = bf16[16,48,256]{2,1,0:T(8,128)(2,1)S(1)} async-done(((bf16[16,48,256]{2,1,0:T(8,128)(2,1)}), bf16[16,48,256]{2,1,0:T(8,128)(2,1)S(1)}, u32[]{:S(2)}, u32[]{:S(2)}) %all-to-all-start.6) | async-done | bytes 393248 | tf_op jit(solution)/shard_map/all_to_all | solution.py:39
  213.8 0.7 copy-done.5
  215.2 2.6 %copy-done = bf16[3072,896]{1,0:T(8,128)(2,1)S(1)} copy-done((bf16[3072,896]{1,0:T(8,128)(2,1)S(1)}, bf16[3072,896]{1,0:T(8,128)(2,1)}, u32[]{:S(2)}) %copy-start) | copy-done | bytes 5505048
  217.8 5.3 %shard_map.261 = (f32[768,3072]{1,0:T(8,128)}, f32[3072,768]{1,0:T(8,128)}, f32[768,768]{1,0:T(8,128)}, f32[16,48,32]{2,1,0:T(8,128)S(1)}) custom-call(s32[4]{0:T(128)S(1)} %pad_add_fusion.1.me_ref, bf16[64,48,896]{2,1,0:T(8,128)(2,1)S(1)} %bitcast.77), custom_call_target="tpu_custom_call" | custom-call | bytes 20971520 | tf_op jit(solution)/shard_map/pallas_call | solution.py:178
  223.1 6.1 %shard_map.262 = bf16[256,768]{1,0:T(8,128)(2,1)} custom-call(bf16[16,48,256]{2,1,0:T(8,128)(2,1)} %copy-done.5, f32[48,768]{1,0:T(8,128)} %get-tuple-element.74.routed_ref, f32[48,768]{1,0:T(8,128)} %get-tuple-element.115.hidden_ref, f32[48,1]{1,0:T(8,128)} %get-tuple-element.116.logit_ref, s32[1,48]{1,0:T(1,128)} %bitcast.92, bf16[256,768]{1,0:T(8,128)(2,1)} %bitcast.86, ...), custom_call_target="tpu_custom_call" | custom-call | flops 169869312 | bytes 6291456 | tf_op jit(solution)/shard_map/pallas_call | solution.py:619
  229.2 5.3 %shard_map.263 = (f32[768,3072]{1,0:T(8,128)}, f32[3072,768]{1,0:T(8,128)}, f32[768,768]{1,0:T(8,128)}, f32[16,48,32]{2,1,0:T(8,128)S(1)}) custom-call(s32[4]{0:T(128)S(1)} %pad_add_fusion.1.me_ref, bf16[64,48,896]{2,1,0:T(8,128)(2,1)S(1)} %collective-permute-done.11.units_in, ...), custom_call_target="tpu_custom_call", output_to_operand_aliasing={{0}: (2, {}), {1}: (3, {}), {2}: (4, {})} | custom-call | bytes 20971520 | tf_op jit(solution)/shard_map/pallas_call | solution.py:178
  (95 shorter events, 10.9 us)
Async XLA Ops:
  13.1 15.9 %copy-start.6 = (f32[48,768]{1,0:T(8,128)S(1)}, f32[48,768]{1,0:T(8,128)}, u32[]{:S(2)}) copy-start(f32[48,768]{1,0:T(8,128)} %get-tuple-element.74.routed_ref) | copy-start | bytes 442372
  13.1 15.9 %copy-start.14 = (f32[768]{0:T(1024)S(1)}, f32[768]{0:T(1024)}, u32[]{:S(2)}) copy-start(f32[768]{0:T(1024)} %router_ref.1) | copy-start | bytes 9220
  13.1 16.0 %copy-start.4 = (bf16[1,256,768]{2,1,0:T(8,128)(2,1)S(1)}, bf16[1,256,768]{2,1,0:T(8,128)(2,1)}, u32[]{:S(2)}) copy-start(bf16[1,256,768]{2,1,0:T(8,128)(2,1)} %param.28) | copy-start | bytes 1179652
  13.1 16.0 %copy-start.16 = (s32[1,1,48]{2,1,0:T(1,128)S(1)}, s32[1,1,48]{2,1,0:T(1,128)}, u32[]{:S(2)}) copy-start(s32[1,1,48]{2,1,0:T(1,128)} %param.30) | copy-start | bytes 580
  13.1 37.6 %all-to-all-start = ((bf16[64,48,256]{2,1,0:T(8,128)(2,1)}), bf16[64,48,256]{2,1,0:T(8,128)(2,1)S(1)}, u32[]{:S(2)}, u32[]{:S(2)}) async-start(bf16[64,48,256]{2,1,0:T(8,128)(2,1)} %bitcast.83), calls=%async_computation | async-start | bytes 3145728 | tf_op jit(solution)/shard_map/all_to_all | solution.py:39
  25.8 75.4 %all-gather.4.cloned.1.call-start = ((), (), s32[]{:S(2)}) async-start(), calls=%async_computation.7 | async-start | bytes 1253376 | tf_op jit(solution)/shard_map/all_gather | solution.py:685
  30.1 29.5 %copy-start.8 = (bf16[48,768]{1,0:T(8,128)(2,1)}, bf16[48,768]{1,0:T(8,128)(2,1)S(1)}, u32[]{:S(2)}) copy-start(bf16[48,768]{1,0:T(8,128)(2,1)S(1)} %get-tuple-element.154.low_ref) | copy-start | bytes 221188
  55.3 0.7 copy-start.1
  56.0 11.8 %all-to-all-start.1 = ((bf16[16,48,128]{2,1,0:T(8,128)(2,1)}), bf16[16,48,128]{2,1,0:T(8,128)(2,1)S(1)}, u32[]{:S(2)}, u32[]{:S(2)}) async-start(bf16[16,48,128]{2,1,0:T(8,128)(2,1)} %bitcast.7), calls=%async_computation.1 | async-start | bytes 393216 | tf_op jit(solution)/shard_map/all_to_all | solution.py:39
  59.5 4.7 %copy-start.17 = (f32[768]{0:T(1024)S(1)}, f32[768]{0:T(1024)}, u32[]{:S(2)}) copy-start(f32[768]{0:T(1024)} %param.24) | copy-start | bytes 9220
  59.5 5.2 %copy-start.18 = (f32[768]{0:T(1024)S(1)}, f32[768]{0:T(1024)}, u32[]{:S(2)}) copy-start(f32[768]{0:T(1024)} %param.25) | copy-start | bytes 9220
  67.8 0.7 copy-start.7
  76.7 3.1 %collective-permute-start = (bf16[4,48,2112]{2,1,0:T(8,128)(2,1)}, bf16[4,48,2112]{2,1,0:T(8,128)(2,1)S(1)}, u32[]{:S(2)}, u32[]{:S(2)}) collective-permute-start(bf16[4,48,2112]{2,1,0:T(8,128)(2,1)} %get-tuple-element.76), channel_id=1, source_target_pairs={{0,2},{2,0},{1,3},{3,1},{4,6},{6,4},{5,7},{7,5},{8,10},{10,8},{9,1... | collective-permute-start | bytes 2433032 | tf_op jit(solution)/shard_map/ppermute | solution.py:713
  80.0 12.9 %copy-start.15 = (f32[3,768]{1,0:T(4,128)S(1)}, f32[3,768]{1,0:T(4,128)}, u32[]{:S(2)}) copy-start(f32[3,768]{1,0:T(4,128)} %get-tuple-element.85) | copy-start | bytes 27652
  81.0 20.1 %collective-permute-start.3 = (bf16[96,2112]{1,0:T(8,128)(2,1)}, bf16[96,2112]{1,0:T(8,128)(2,1)S(1)}, u32[]{:S(2)}, u32[]{:S(2)}) collective-permute-start(bf16[96,2112]{1,0:T(8,128)(2,1)} %get-tuple-element.138), channel_id=1, source_target_pairs={{0,48},{2,14},{4,52},{6,2},{8,56},{10,6},{12,60},{14,10},{16,0},{1... | collective-permute-start | bytes 1216520 | tf_op jit(solution)/shard_map/ppermute | solution.py:74
  82.5 18.7 %collective-permute-start.2 = (bf16[96,2112]{1,0:T(8,128)(2,1)}, bf16[96,2112]{1,0:T(8,128)(2,1)S(1)}, u32[]{:S(2)}, u32[]{:S(2)}) collective-permute-start(bf16[96,2112]{1,0:T(8,128)(2,1)} %get-tuple-element.139), channel_id=1, source_target_pairs={{0,32},{2,10},{4,36},{6,14},{8,40},{10,2},{12,44},{14,6},{16,48},{... | collective-permute-start | bytes 1216520 | tf_op jit(solution)/shard_map/ppermute | solution.py:74
  82.7 18.4 %collective-permute-start.1 = (bf16[96,2112]{1,0:T(8,128)(2,1)}, bf16[96,2112]{1,0:T(8,128)(2,1)S(1)}, u32[]{:S(2)}, u32[]{:S(2)}) collective-permute-start(bf16[96,2112]{1,0:T(8,128)(2,1)} %get-tuple-element.140), channel_id=1, source_target_pairs={{0,16},{2,6},{4,20},{6,10},{8,24},{10,14},{12,28},{14,2},{16,32},{... | collective-permute-start | bytes 1216520 | tf_op jit(solution)/shard_map/ppermute | solution.py:74
  83.0 18.1 %all-to-all-start.2 = ((bf16[16,48,128]{2,1,0:T(8,128)(2,1)}), bf16[16,48,128]{2,1,0:T(8,128)(2,1)}, u32[]{:S(2)}, u32[]{:S(2)}) async-start(bf16[16,48,128]{2,1,0:T(8,128)(2,1)} %get-tuple-element.77), calls=%async_computation.2 | async-start | bytes 393216 | tf_op jit(solution)/shard_map/all_to_all | solution.py:39
  92.8 121.0 %all-gather.6.cloned.1.call-start = ((), (), s32[]{:S(2)}) async-start(), calls=%async_computation.8 | async-start | bytes 5591040 | tf_op jit(solution)/shard_map/all_gather | solution.py:742
  102.8 4.5 %copy-start.2 = (f32[2,384,64]{2,1,0:T(8,128)S(1)}, f32[2,384,64]{2,1,0:T(8,128)}, u32[]{:S(2)}) copy-start(f32[2,384,64]{2,1,0:T(8,128)} %copy-done.1) | copy-start | bytes 589828
  103.0 10.3 %collective-permute-start.6 = (bf16[4,48,896]{2,1,0:T(8,128)(2,1)S(1)}, bf16[4,48,896]{2,1,0:T(8,128)(2,1)S(1)}, u32[]{:S(2)}, u32[]{:S(2)}) collective-permute-start(bf16[4,48,896]{2,1,0:T(8,128)(2,1)S(1)} %get-tuple-element.142), channel_id=1, source_target_pairs={{0,12},{2,50},{4,0},{6,54},{8,4},{10,58},{12,8},{14,62},{16,28},{1... | collective-permute-start | bytes 1032200 | tf_op jit(solution)/shard_map/ppermute | solution.py:74
  105.4 7.9 %collective-permute-start.5 = (bf16[4,48,896]{2,1,0:T(8,128)(2,1)S(1)}, bf16[4,48,896]{2,1,0:T(8,128)(2,1)S(1)}, u32[]{:S(2)}, u32[]{:S(2)}) collective-permute-start(bf16[4,48,896]{2,1,0:T(8,128)(2,1)S(1)} %get-tuple-element.143), channel_id=1, source_target_pairs={{0,8},{2,34},{4,12},{6,38},{8,0},{10,42},{12,4},{14,46},{16,24},{1... | collective-permute-start | bytes 1032200 | tf_op jit(solution)/shard_map/ppermute | solution.py:74
  107.4 9.6 %collective-permute-start.4 = (bf16[4,48,896]{2,1,0:T(8,128)(2,1)S(1)}, bf16[4,48,896]{2,1,0:T(8,128)(2,1)S(1)}, u32[]{:S(2)}, u32[]{:S(2)}) collective-permute-start(bf16[4,48,896]{2,1,0:T(8,128)(2,1)S(1)} %get-tuple-element.144), channel_id=1, source_target_pairs={{0,4},{2,18},{4,8},{6,22},{8,12},{10,26},{12,0},{14,30},{16,20},{1... | collective-permute-start | bytes 1032200 | tf_op jit(solution)/shard_map/ppermute | solution.py:74
  117.2 4.6 %collective-permute-start.7 = (bf16[48,896]{1,0:T(8,128)(2,1)S(1)}, bf16[48,896]{1,0:T(8,128)(2,1)S(1)}, u32[]{:S(2)}, u32[]{:S(2)}) collective-permute-start(bf16[48,896]{1,0:T(8,128)(2,1)S(1)} %get-tuple-element.148), channel_id=1, source_target_pairs={{0,1},{1,64},{64,65},{65,0},{2,3},{3,66},{66,67},{67,2},{4,5},{5,6... | collective-permute-start | bytes 258056 | tf_op jit(solution)/shard_map/ppermute | solution.py:74
  117.6 4.3 %collective-permute-start.9 = (bf16[48,896]{1,0:T(8,128)(2,1)S(1)}, bf16[48,896]{1,0:T(8,128)(2,1)S(1)}, u32[]{:S(2)}, u32[]{:S(2)}) collective-permute-start(bf16[48,896]{1,0:T(8,128)(2,1)S(1)} %get-tuple-element.149), channel_id=1, source_target_pairs={{0,65},{1,0},{64,1},{65,64},{2,67},{3,2},{66,3},{67,66},{4,69},{5,... | collective-permute-start | bytes 258056 | tf_op jit(solution)/shard_map/ppermute | solution.py:74
  120.0 4.8 %collective-permute-start.8 = (bf16[48,896]{1,0:T(8,128)(2,1)S(1)}, bf16[48,896]{1,0:T(8,128)(2,1)S(1)}, u32[]{:S(2)}, u32[]{:S(2)}) collective-permute-start(bf16[48,896]{1,0:T(8,128)(2,1)S(1)} %get-tuple-element.150), channel_id=1, source_target_pairs={{0,64},{1,65},{64,0},{65,1},{2,66},{3,67},{66,2},{67,3},{4,68},{5,... | collective-permute-start | bytes 258056 | tf_op jit(solution)/shard_map/ppermute | solution.py:74
  144.3 5.2 %copy-start.9 = (bf16[48,3072]{1,0:T(8,128)(2,1)S(1)}, bf16[48,3072]{1,0:T(8,128)(2,1)}, u32[]{:S(2)}) copy-start(bf16[48,3072]{1,0:T(8,128)(2,1)} %get-tuple-element.99) | copy-start | bytes 884740
  144.3 5.2 %copy-start.10 = (f32[48,768]{1,0:T(8,128)S(1)}, f32[48,768]{1,0:T(8,128)}, u32[]{:S(2)}) copy-start(f32[48,768]{1,0:T(8,128)} %get-tuple-element.98) | copy-start | bytes 442372
  145.6 13.7 %all-to-all-start.4 = ((bf16[32,32,192]{2,1,0:T(8,128)(2,1)}), bf16[32,32,192]{2,1,0:T(8,128)(2,1)S(1)}, u32[]{:S(2)}, u32[]{:S(2)}) async-start(bf16[32,32,192]{2,1,0:T(8,128)(2,1)} %pad_maximum_fusion), calls=%async_computation.4 | async-start | bytes 1048576 | tf_op jit(solution)/shard_map/all_to_all | solution.py:39
  149.5 3.3 %copy-start.3 = (bf16[1,256,768]{2,1,0:T(8,128)(2,1)S(1)}, bf16[1,256,768]{2,1,0:T(8,128)(2,1)}, u32[]{:S(2)}) copy-start(bf16[1,256,768]{2,1,0:T(8,128)(2,1)} %param.16) | copy-start | bytes 1179652
  190.4 9.6 %collective-permute-start.10 = (bf16[64,24,640]{2,1,0:T(8,128)(2,1)S(1)}, bf16[64,24,640]{2,1,0:T(8,128)(2,1)}, u32[]{:S(2)}, u32[]{:S(2)}) collective-permute-start(bf16[64,24,640]{2,1,0:T(8,128)(2,1)S(1)} %all_to_all.36.own_ref), channel_id=1, source_target_pairs={{0,2},{2,0},{1,3},{3,1},{4,6},{6,4},{5,7},{7,5},{8,10},{10,8},{9,1... | collective-permute-start | bytes 5898248 | tf_op jit(solution)/shard_map/ppermute | solution.py:774
  196.5 17.3 %all-to-all-start.6 = ((bf16[16,48,256]{2,1,0:T(8,128)(2,1)}), bf16[16,48,256]{2,1,0:T(8,128)(2,1)S(1)}, u32[]{:S(2)}, u32[]{:S(2)}) async-start(bf16[16,48,256]{2,1,0:T(8,128)(2,1)} %bitcast.37), calls=%async_computation.6 | async-start | bytes 786432 | tf_op jit(solution)/shard_map/all_to_all | solution.py:39
  199.9 6.1 %copy-start.11 = (f32[768]{0:T(1024)S(1)}, f32[768]{0:T(1024)}, u32[]{:S(2)}) copy-start(f32[768]{0:T(1024)} %gain_ref.3) | copy-start | bytes 9220
  199.9 6.1 %copy-start.12 = (f32[768]{0:T(1024)S(1)}, f32[768]{0:T(1024)}, u32[]{:S(2)}) copy-start(f32[768]{0:T(1024)} %bias_ref.1) | copy-start | bytes 9220
  206.1 17.1 %copy-start.13 = (f32[768]{0:T(1024)}, f32[768]{0:T(1024)S(1)}, u32[]{:S(2)}) copy-start(f32[768]{0:T(1024)S(1)} %get-tuple-element.129) | copy-start | bytes 9220
  213.8 0.7 copy-start.5
  214.5 14.7 %collective-permute-start.11 = (bf16[64,48,896]{2,1,0:T(8,128)(2,1)}, bf16[64,48,896]{2,1,0:T(8,128)(2,1)S(1)}, u32[]{:S(2)}, u32[]{:S(2)}) collective-permute-start(bf16[64,48,896]{2,1,0:T(8,128)(2,1)} %bitcast.76), channel_id=1, source_target_pairs={{0,2},{2,0},{1,3},{3,1},{4,6},{6,4},{5,7},{7,5},{8,10},{10,8},{9,1... | collective-permute-start | bytes 16515080 | tf_op jit(solution)/shard_map/ppermute | solution.py:79
  215.2 2.6 %copy-start = (bf16[3072,896]{1,0:T(8,128)(2,1)S(1)}, bf16[3072,896]{1,0:T(8,128)(2,1)}, u32[]{:S(2)}) copy-start(bf16[3072,896]{1,0:T(8,128)(2,1)} %all-gather.6.cloned.1.call-done) | copy-start | bytes 16515076
Sparse Core Ops, SparseCore 0:
  29.1 48.5 all-gather.3
  125.6 86.4 all-gather.5

commit v2 on v1

--- a/solution.py
+++ b/solution.py
@@ -747,20 +747,19 @@
     ).astype(BF16)
 
     grad_qkv = mm_tn(normed_block, grad_heads).astype(BF16).reshape(32, 24, 3 * HEAD)
-    column_sum = jnp.sum(grad_heads.astype(F32), axis=0).astype(BF16)
-    column_sum = jnp.broadcast_to(column_sum[None, None, :], (32, 8, 3 * HEAD))
-    grad_qkv = swap(jnp.concatenate([grad_qkv, column_sum], axis=1), ("x", "z", "yl"))
+    column_sum = jnp.sum(grad_heads.astype(F32), axis=0).astype(BF16).reshape(1, 3, HEAD)
+    column_sum = jnp.broadcast_to(jnp.pad(column_sum, ((0, 0), (0, 21), (0, 0))), (32, 24, HEAD))
+    grad_qkv = swap(jnp.concatenate([grad_qkv, column_sum], axis=2), ("x", "z", "yl"))
     grad_qkv, output = lax.optimization_barrier((grad_qkv, output))
-    grad_qkv = jnp.sum(grad_qkv.reshape(4, 4, 2, 32, 3 * HEAD)[:, :3].astype(F32), axis=(0, 2))
+    grad_qkv = jnp.sum(grad_qkv.reshape(4, 4, 2, 24, 4 * HEAD)[:, :3].astype(F32), axis=(0, 2))
+    column_sum = grad_qkv[:, :3, 3 * HEAD :].transpose(1, 0, 2).reshape(9 * HEAD)
     grad_qkv = jnp.concatenate(
         [
-            grad_qkv[:, :, kind * HEAD : (kind + 1) * HEAD].transpose(1, 0, 2).reshape(32, 3 * HEAD)
+            grad_qkv[:, :, kind * HEAD : (kind + 1) * HEAD].transpose(1, 0, 2).reshape(24, 3 * HEAD)
             for kind in range(3)
         ],
         axis=1,
     )
-    column_sum = grad_qkv[24]
-    grad_qkv = grad_qkv[:24]
     norm_sums = jnp.stack(
         [jnp.sum(w_part * grad_qkv, axis=1), jnp.sum(w_part * column_sum[None, :], axis=1)], axis=1
     )

time: 243 us -> 243 us (level)
  no operation moved by 1% of the time
where the time goes in v2:
time: 243 us; the launch traced here: 242 us
  waiting for transfers between devices  50.8 us (21%)
  starting transfers between devices  49.4 us (20%)
  Pallas kernels  47.4 us (20%)
  blocking collectives  46.8 us (19%)
  local copies, waits for them, and re-layouts  16.8 us (7%)
  between operations  15.2 us (6%)
  matrix products  11.9 us (5%)
  other arithmetic  4.01 us (2%)
    all_to_all x2, blocking collectives, swap(): return lax.all_to_all(parts, axes, split_axis=0, concat_axis=0, tiled=True)  46.8 us
    all_to_all x5, waiting for transfers between devices, swap(): return lax.all_to_all(parts, axes, split_axis=0, concat_axis=0, tiled=True)  40.5 us
    all_to_all x5, starting transfers between devices, swap(): return lax.all_to_all(parts, axes, split_axis=0, concat_axis=0, tiled=True)  33.2 us
    dot_general x5, matrix products, dot(): lax.dot_general(left, right, (dims, ((), ())), precision=precision, prefe...  11.9 us
    pallas_call x2, Pallas kernels, place(): pl.pallas_call(functools.partial(place_kernel, 1 if before else 0), out_s...  10.6 us
    ppermute x9, starting transfers between devices, ring_swap(): mine.append(lax.ppermute(part, axes, pairs_of(step)))  9.13 us
    ppermute x9, waiting for transfers between devices, ring_swap(): mine.append(lax.ppermute(part, axes, pairs_of(step)))  8.57 us
    pallas_call x1, Pallas kernels, feed(): pl.pallas_call(feed_kernel, out_shape=(jax.ShapeDtypeStruct((4, SLOTS, 2...  8.28 us
  transfers between devices with their start and end apart: 19, of which 10 were waited for; matrix products, arithmetic and copies ran while one was open for 10% of the time, Pallas kernels for 15%

profile of v2, /device:TPU:1, one launch (start us, length us, event | category | flops | bytes accessed | tf_op | source)
XLA Modules:
  0.0 242.3 jit_solution(12657486657243934719)
XLA Ops:
  8.4 4.7 %shard_map.255 = (bf16[4,16,48,256]{3,2,1,0:T(8,128)(2,1)}, bf16[48,768]{1,0:T(8,128)(2,1)}, f32[48,768]{1,0:T(8,128)}) custom-call(s32[2]{0:T(128)} %pad_add_fusion.count_ref, s32[1,48]{1,0:T(1,128)} %bitcast.95, s32[1,256]{1,0:T(1,128)} %ids_ref.1, bf16[256,768]{1,0:T(8,128)(2,1)} %bitcast.87, f32[768]{0:T(1024)} %gain_ref.3, f32[768]{0:T(1024)} %bias_ref.1, ...), custom_call_target="tpu_custom_call" | custom-call | flops 169869312 | bytes 6291456 | tf_op jit(solution)/shard_map/pallas_call | solution.py:287
  13.1 12.6 %all-to-all-start = ((bf16[64,48,256]{2,1,0:T(8,128)(2,1)}), bf16[64,48,256]{2,1,0:T(8,128)(2,1)S(1)}, u32[]{:S(2)}, u32[]{:S(2)}) async-start(bf16[64,48,256]{2,1,0:T(8,128)(2,1)} %bitcast.86), calls=%async_computation | async-start | bytes 3145728 | tf_op jit(solution)/shard_map/all_to_all | solution.py:39
  26.5 0.8 dynamic_slice.50
  27.3 0.8 dynamic_slice.48
  28.1 0.8 dynamic_slice.49
  29.2 0.9 fusion.12
  30.1 20.7 %all-to-all-done = bf16[64,48,256]{2,1,0:T(8,128)(2,1)S(1)} async-done(((bf16[64,48,256]{2,1,0:T(8,128)(2,1)}), bf16[64,48,256]{2,1,0:T(8,128)(2,1)S(1)}, u32[]{:S(2)}, u32[]{:S(2)}) %all-to-all-start) | async-done | bytes 1572896 | tf_op jit(solution)/shard_map/all_to_all | solution.py:39
  50.8 4.5 %shard_map.256 = (f32[2,384,64]{2,1,0:T(8,128)S(1)}, bf16[2,384,128]{2,1,0:T(8,128)(2,1)}, f32[2,1,384]{2,1,0:T(1,128)S(1)}) custom-call(s32[1]{0:T(128)} %bitcast.x_ref, bf16[4,2,384,256]{3,2,1,0:T(8,128)(2,1)S(1)} %bitcast.82), custom_call_target="tpu_custom_call" | custom-call | flops 3623878656 | bytes 3145728 | tf_op jit(solution)/shard_map/pallas_call | solution.py:362
  55.3 0.7 copy-done.1
  56.0 3.5 %all-to-all-start.1 = ((bf16[16,48,128]{2,1,0:T(8,128)(2,1)}), bf16[16,48,128]{2,1,0:T(8,128)(2,1)S(1)}, u32[]{:S(2)}, u32[]{:S(2)}) async-start(bf16[16,48,128]{2,1,0:T(8,128)(2,1)} %bitcast.7), calls=%async_computation.1 | async-start | bytes 393216 | tf_op jit(solution)/shard_map/all_to_all | solution.py:39
  59.6 4.6 %fusion.13.grad_act_ref = f32[48,3072]{1,0:T(8,128)} fusion(bf16[48,768]{1,0:T(8,128)(2,1)S(1)} %get-tuple-element.154.low_ref, bf16[3072,768]{1,0:T(8,128)(2,1)} %param.27), kind=kOutput, calls=%fused_computation.61 | convolution fusion | flops 226492416 | bytes 5382144 | tf_op jit(solution)/shard_map/dot_general | solution.py:83
  66.1 1.7 all-to-all-done.1.parts_ref
  68.4 8.3 %shard_map.257 = (bf16[4,48,2112]{2,1,0:T(8,128)(2,1)}, bf16[4,48,2112]{2,1,0:T(8,128)(2,1)}, bf16[16,48,128]{2,1,0:T(8,128)(2,1)}, f32[48,768]{1,0:T(8,128)}, f...) custom-call(bf16[16,48,128]{2,1,0:T(8,128)(2,1)} %copy-done.7, ...), custom_call_target="tpu_custom_call" | custom-call | flops 566231040 | bytes 10485760 | tf_op jit(solution)/shard_map/pallas_call | solution.py:523
  76.7 0.9 collective-permute-start
  77.7 1.2 constant_dynamic-update-slice_fusion.1
  78.9 1.0 collective-permute-done
  80.0 1.1 dynamic-slice_bitcast_fusion
  81.0 1.4 collective-permute-start.3
  83.0 9.8 %all-to-all-start.2 = ((bf16[16,48,128]{2,1,0:T(8,128)(2,1)}), bf16[16,48,128]{2,1,0:T(8,128)(2,1)}, u32[]{:S(2)}, u32[]{:S(2)}) async-start(bf16[16,48,128]{2,1,0:T(8,128)(2,1)} %get-tuple-element.77), calls=%async_computation.2 | async-start | bytes 393216 | tf_op jit(solution)/shard_map/all_to_all | solution.py:39
  92.9 1.0 reshape.134
  93.9 1.0 pad.17.refs_4_
  94.9 6.2 %all-to-all-done.2 = bf16[16,48,128]{2,1,0:T(8,128)(2,1)} async-done(((bf16[16,48,128]{2,1,0:T(8,128)(2,1)}), bf16[16,48,128]{2,1,0:T(8,128)(2,1)}, u32[]{:S(2)}, u32[]{:S(2)}) %all-to-all-start.2) | async-done | bytes 196640 | tf_op jit(solution)/shard_map/all_to_all | solution.py:39
  101.2 1.6 shard_map.258
  103.0 2.4 %collective-permute-start.6 = (bf16[4,48,896]{2,1,0:T(8,128)(2,1)S(1)}, bf16[4,48,896]{2,1,0:T(8,128)(2,1)S(1)}, u32[]{:S(2)}, u32[]{:S(2)}) collective-permute-start(bf16[4,48,896]{2,1,0:T(8,128)(2,1)S(1)} %get-tuple-element.142), channel_id=1, source_target_pairs={{0,12},{2,50},{4,0},{6,54},{8,4},{10,58},{12,8},{14,62},{16,28},{1... | collective-permute-start | bytes 1032200 | tf_op jit(solution)/shard_map/ppermute | solution.py:74
  105.4 2.0 collective-permute-start.5
  107.4 5.9 %shard_map.259 = (bf16[2,384,64]{2,1,0:T(8,128)(2,1)S(1)}, bf16[4,2,384,128]{3,2,1,0:T(8,128)(2,1)S(1)}) custom-call(s32[1]{0:T(128)} %bitcast.x_ref, bf16[4,2,384,256]{3,2,1,0:T(8,128)(2,1)S(1)} %bitcast.83, bf16[2,384,128]{2,1,0:T(8,128)(2,1)} %bitcast.21.do_ref, f32[2,384,64]{2,1,0:T(8,128)S(1)} %copy-done.2, f32[2,1,384]{2,1,0:T(1,128)S(1)} %get-tuple-element.89.lse_ref), custom_call_target="tpu_custom_call" | custom-call | flops 9059696640 | bytes 6291456 | tf_op jit(solution)/shard_map/pallas_call | solution.py:422
  113.3 3.6 %collective-permute-done.4 = bf16[4,48,896]{2,1,0:T(8,128)(2,1)S(1)} collective-permute-done((bf16[4,48,896]{2,1,0:T(8,128)(2,1)S(1)}, bf16[4,48,896]{2,1,0:T(8,128)(2,1)S(1)}, u32[]{:S(2)}, u32[]{:S(2)}) %collective-permute-start.4) | collective-permute-done | bytes 344096 | tf_op jit(solution)/shard_map/ppermute | solution.py:74
  117.6 2.4 collective-permute-start.9
  120.0 1.9 collective-permute-done.7
  121.9 2.9 %collective-permute-done.8 = bf16[48,896]{1,0:T(8,128)(2,1)S(1)} collective-permute-done((bf16[48,896]{1,0:T(8,128)(2,1)S(1)}, bf16[48,896]{1,0:T(8,128)(2,1)S(1)}, u32[]{:S(2)}, u32[]{:S(2)}) %collective-permute-start.8) | collective-permute-done | bytes 86048 | tf_op jit(solution)/shard_map/ppermute | solution.py:74
  125.5 16.9 %all_to_all.35 = bf16[4,2,384,128]{3,2,1,0:T(8,128)(2,1)S(1)} all-to-all(bf16[4,2,384,128]{3,2,1,0:T(8,128)(2,1)S(1)} %get-tuple-element.96), channel_id=1, replica_groups=mesh['yh'=2,'x'=4,'z'=4,'c'=2,'yl'=2] {'x'}, dimensions={0} | all-to-all | bytes 1572864 | tf_op jit(solution)/shard_map/all_to_all | solution.py:39
  142.9 1.8 convolution_convert_fusion
  144.9 0.9 pad_maximum_fusion.1
  145.8 3.9 %all-to-all-start.4 = ((bf16[32,24,256]{2,1,0:T(8,128)(2,1)}), bf16[32,24,256]{2,1,0:T(8,128)(2,1)S(1)}, u32[]{:S(2)}, u32[]{:S(2)}) async-start(bf16[32,24,256]{2,1,0:T(8,128)(2,1)} %pad_maximum_fusion.1), calls=%async_computation.4 | async-start | bytes 786432 | tf_op jit(solution)/shard_map/all_to_all | solution.py:39
  149.7 3.3 %fusion.1 = f32[48,768]{1,0:T(8,128)S(1)} fusion(f32[48,768]{1,0:T(8,128)S(1)} %copy-done.10, bf16[48,3072]{1,0:T(8,128)(2,1)S(1)} %copy-done.9, bf16[3072,768]{1,0:T(8,128)(2,1)} %param.27, f32[48]{0:T(128)S(1)} %get-tuple-element.136), kind=kOutput, calls=%fused_computation.4 | convolution fusion | flops 226566144 | bytes 5308608 | tf_op jit(solution)/shard_map/dot_general | solution.py:83
  153.0 1.3 fusion
  154.3 4.3 %all-to-all-done.4 = bf16[32,24,256]{2,1,0:T(8,128)(2,1)S(1)} async-done(((bf16[32,24,256]{2,1,0:T(8,128)(2,1)}), bf16[32,24,256]{2,1,0:T(8,128)(2,1)S(1)}, u32[]{:S(2)}, u32[]{:S(2)}) %all-to-all-start.4) | async-done | bytes 393248 | tf_op jit(solution)/shard_map/all_to_all | solution.py:39
  159.9 29.9 %all_to_all.36.own_ref = bf16[64,24,640]{2,1,0:T(8,128)(2,1)S(1)} all-to-all(bf16[64,24,640]{2,1,0:T(8,128)(2,1)S(1)} %broadcast_in_dim.49), channel_id=1, replica_groups=mesh['yh'=2,'x'=4,'z'=4,'c'=2,'yl'=2] {'x','yh','yl','z'}, dimensions={0} | all-to-all | bytes 3932160 | tf_op jit(solution)/shard_map/all_to_all | solution.py:39
  189.8 5.0 %collective-permute-start.10 = (bf16[64,24,640]{2,1,0:T(8,128)(2,1)S(1)}, bf16[64,24,640]{2,1,0:T(8,128)(2,1)}, u32[]{:S(2)}, u32[]{:S(2)}) collective-permute-start(bf16[64,24,640]{2,1,0:T(8,128)(2,1)S(1)} %all_to_all.36.own_ref), channel_id=1, source_target_pairs={{0,2},{2,0},{1,3},{3,1},{4,6},{6,4},{5,7},{7,5},{8,10},{10,8},{9,1... | collective-permute-start | bytes 5898248 | tf_op jit(solution)/shard_map/ppermute | solution.py:773
  194.9 0.8 pad.20
  195.7 3.5 %all-to-all-start.6 = ((bf16[16,48,256]{2,1,0:T(8,128)(2,1)}), bf16[16,48,256]{2,1,0:T(8,128)(2,1)S(1)}, u32[]{:S(2)}, u32[]{:S(2)}) async-start(bf16[16,48,256]{2,1,0:T(8,128)(2,1)} %bitcast.39), calls=%async_computation.6 | async-start | bytes 786432 | tf_op jit(solution)/shard_map/all_to_all | solution.py:39
  199.2 5.7 %shard_map.260 = (f32[768,768]{1,0:T(8,128)}, f32[768,768]{1,0:T(8,128)}, f32[768,768]{1,0:T(8,128)}, f32[768,64]{1,0:T(8,128)S(1)}) custom-call(s32[4]{0:T(128)S(1)} %pad_add_fusion.1.me_ref, bf16[64,24,640]{2,1,0:T(8,128)(2,1)S(1)} %all_to_all.36.own_ref, bf16[64,24,640]{2,1,0:T(8,128)(2,1)} %collective-permute-done.10.other_ref), custom_call_target="tpu_custom_call" | custom-call | bytes 12582912 | tf_op jit(solution)/shard_map/pallas_call | solution.py:228
  206.0 7.5 %all-to-all-done.6.back_ref = bf16[16,48,256]{2,1,0:T(8,128)(2,1)S(1)} async-done(((bf16[16,48,256]{2,1,0:T(8,128)(2,1)}), bf16[16,48,256]{2,1,0:T(8,128)(2,1)S(1)}, u32[]{:S(2)}, u32[]{:S(2)}) %all-to-all-start.6) | async-done | bytes 393248 | tf_op jit(solution)/shard_map/all_to_all | solution.py:39
  214.3 1.0 collective-permute-start.11
  215.3 2.6 %copy-done = bf16[3072,896]{1,0:T(8,128)(2,1)S(1)} copy-done((bf16[3072,896]{1,0:T(8,128)(2,1)S(1)}, bf16[3072,896]{1,0:T(8,128)(2,1)}, u32[]{:S(2)}) %copy-start) | copy-done | bytes 5505048
  217.8 5.3 %shard_map.261 = (f32[768,3072]{1,0:T(8,128)}, f32[3072,768]{1,0:T(8,128)}, f32[768,768]{1,0:T(8,128)}, f32[16,48,32]{2,1,0:T(8,128)S(1)}) custom-call(s32[4]{0:T(128)S(1)} %pad_add_fusion.1.me_ref, bf16[64,48,896]{2,1,0:T(8,128)(2,1)S(1)} %bitcast.81), custom_call_target="tpu_custom_call" | custom-call | bytes 20971520 | tf_op jit(solution)/shard_map/pallas_call | solution.py:178
  223.1 6.1 %shard_map.262 = bf16[256,768]{1,0:T(8,128)(2,1)} custom-call(bf16[16,48,256]{2,1,0:T(8,128)(2,1)} %copy-done.5, f32[48,768]{1,0:T(8,128)} %get-tuple-element.74.routed_ref, f32[48,768]{1,0:T(8,128)} %get-tuple-element.115.hidden_ref, f32[48,1]{1,0:T(8,128)} %get-tuple-element.116.logit_ref, s32[1,48]{1,0:T(1,128)} %bitcast.96, bf16[256,768]{1,0:T(8,128)(2,1)} %bitcast.89, ...), custom_call_target="tpu_custom_call" | custom-call | flops 169869312 | bytes 6291456 | tf_op jit(solution)/shard_map/pallas_call | solution.py:619
  229.3 5.3 %shard_map.263 = (f32[768,3072]{1,0:T(8,128)}, f32[3072,768]{1,0:T(8,128)}, f32[768,768]{1,0:T(8,128)}, f32[16,48,32]{2,1,0:T(8,128)S(1)}) custom-call(s32[4]{0:T(128)S(1)} %pad_add_fusion.1.me_ref, bf16[64,48,896]{2,1,0:T(8,128)(2,1)S(1)} %collective-permute-done.11.units_in, ...), custom_call_target="tpu_custom_call", output_to_operand_aliasing={{0}: (2, {}), {1}: (3, {}), {2}: (4, {})} | custom-call | bytes 20971520 | tf_op jit(solution)/shard_map/pallas_call | solution.py:178
  (100 shorter events, 11.0 us)
Async XLA Ops:
  13.1 15.9 %copy-start.6 = (f32[48,768]{1,0:T(8,128)S(1)}, f32[48,768]{1,0:T(8,128)}, u32[]{:S(2)}) copy-start(f32[48,768]{1,0:T(8,128)} %get-tuple-element.74.routed_ref) | copy-start | bytes 442372
  13.1 15.9 %copy-start.14 = (f32[768]{0:T(1024)S(1)}, f32[768]{0:T(1024)}, u32[]{:S(2)}) copy-start(f32[768]{0:T(1024)} %router_ref.1) | copy-start | bytes 9220
  13.1 16.0 %copy-start.4 = (bf16[1,256,768]{2,1,0:T(8,128)(2,1)S(1)}, bf16[1,256,768]{2,1,0:T(8,128)(2,1)}, u32[]{:S(2)}) copy-start(bf16[1,256,768]{2,1,0:T(8,128)(2,1)} %param.28) | copy-start | bytes 1179652
  13.1 16.0 %copy-start.16 = (s32[1,1,48]{2,1,0:T(1,128)S(1)}, s32[1,1,48]{2,1,0:T(1,128)}, u32[]{:S(2)}) copy-start(s32[1,1,48]{2,1,0:T(1,128)} %param.30) | copy-start | bytes 580
  13.1 37.6 %all-to-all-start = ((bf16[64,48,256]{2,1,0:T(8,128)(2,1)}), bf16[64,48,256]{2,1,0:T(8,128)(2,1)S(1)}, u32[]{:S(2)}, u32[]{:S(2)}) async-start(bf16[64,48,256]{2,1,0:T(8,128)(2,1)} %bitcast.86), calls=%async_computation | async-start | bytes 3145728 | tf_op jit(solution)/shard_map/all_to_all | solution.py:39
  25.8 75.4 %all-gather.4.cloned.1.call-start = ((), (), s32[]{:S(2)}) async-start(), calls=%async_computation.7 | async-start | bytes 1253376 | tf_op jit(solution)/shard_map/all_gather | solution.py:685
  30.1 29.5 %copy-start.8 = (bf16[48,768]{1,0:T(8,128)(2,1)}, bf16[48,768]{1,0:T(8,128)(2,1)S(1)}, u32[]{:S(2)}) copy-start(bf16[48,768]{1,0:T(8,128)(2,1)S(1)} %get-tuple-element.154.low_ref) | copy-start | bytes 221188
  55.3 0.7 copy-start.1
  56.0 11.8 %all-to-all-start.1 = ((bf16[16,48,128]{2,1,0:T(8,128)(2,1)}), bf16[16,48,128]{2,1,0:T(8,128)(2,1)S(1)}, u32[]{:S(2)}, u32[]{:S(2)}) async-start(bf16[16,48,128]{2,1,0:T(8,128)(2,1)} %bitcast.7), calls=%async_computation.1 | async-start | bytes 393216 | tf_op jit(solution)/shard_map/all_to_all | solution.py:39
  59.5 4.7 %copy-start.17 = (f32[768]{0:T(1024)S(1)}, f32[768]{0:T(1024)}, u32[]{:S(2)}) copy-start(f32[768]{0:T(1024)} %param.24) | copy-start | bytes 9220
  59.5 5.2 %copy-start.18 = (f32[768]{0:T(1024)S(1)}, f32[768]{0:T(1024)}, u32[]{:S(2)}) copy-start(f32[768]{0:T(1024)} %param.25) | copy-start | bytes 9220
  67.8 0.7 copy-start.7
  76.7 3.1 %collective-permute-start = (bf16[4,48,2112]{2,1,0:T(8,128)(2,1)}, bf16[4,48,2112]{2,1,0:T(8,128)(2,1)S(1)}, u32[]{:S(2)}, u32[]{:S(2)}) collective-permute-start(bf16[4,48,2112]{2,1,0:T(8,128)(2,1)} %get-tuple-element.76), channel_id=1, source_target_pairs={{0,2},{2,0},{1,3},{3,1},{4,6},{6,4},{5,7},{7,5},{8,10},{10,8},{9,1... | collective-permute-start | bytes 2433032 | tf_op jit(solution)/shard_map/ppermute | solution.py:713
  80.0 12.9 %copy-start.15 = (f32[3,768]{1,0:T(4,128)S(1)}, f32[3,768]{1,0:T(4,128)}, u32[]{:S(2)}) copy-start(f32[3,768]{1,0:T(4,128)} %get-tuple-element.85) | copy-start | bytes 27652
  81.0 20.1 %collective-permute-start.3 = (bf16[96,2112]{1,0:T(8,128)(2,1)}, bf16[96,2112]{1,0:T(8,128)(2,1)S(1)}, u32[]{:S(2)}, u32[]{:S(2)}) collective-permute-start(bf16[96,2112]{1,0:T(8,128)(2,1)} %get-tuple-element.138), channel_id=1, source_target_pairs={{0,48},{2,14},{4,52},{6,2},{8,56},{10,6},{12,60},{14,10},{16,0},{1... | collective-permute-start | bytes 1216520 | tf_op jit(solution)/shard_map/ppermute | solution.py:74
  82.5 18.7 %collective-permute-start.2 = (bf16[96,2112]{1,0:T(8,128)(2,1)}, bf16[96,2112]{1,0:T(8,128)(2,1)S(1)}, u32[]{:S(2)}, u32[]{:S(2)}) collective-permute-start(bf16[96,2112]{1,0:T(8,128)(2,1)} %get-tuple-element.139), channel_id=1, source_target_pairs={{0,32},{2,10},{4,36},{6,14},{8,40},{10,2},{12,44},{14,6},{16,48},{... | collective-permute-start | bytes 1216520 | tf_op jit(solution)/shard_map/ppermute | solution.py:74
  82.7 18.4 %collective-permute-start.1 = (bf16[96,2112]{1,0:T(8,128)(2,1)}, bf16[96,2112]{1,0:T(8,128)(2,1)S(1)}, u32[]{:S(2)}, u32[]{:S(2)}) collective-permute-start(bf16[96,2112]{1,0:T(8,128)(2,1)} %get-tuple-element.140), channel_id=1, source_target_pairs={{0,16},{2,6},{4,20},{6,10},{8,24},{10,14},{12,28},{14,2},{16,32},{... | collective-permute-start | bytes 1216520 | tf_op jit(solution)/shard_map/ppermute | solution.py:74
  83.0 18.1 %all-to-all-start.2 = ((bf16[16,48,128]{2,1,0:T(8,128)(2,1)}), bf16[16,48,128]{2,1,0:T(8,128)(2,1)}, u32[]{:S(2)}, u32[]{:S(2)}) async-start(bf16[16,48,128]{2,1,0:T(8,128)(2,1)} %get-tuple-element.77), calls=%async_computation.2 | async-start | bytes 393216 | tf_op jit(solution)/shard_map/all_to_all | solution.py:39
  92.8 120.7 %all-gather.6.cloned.1.call-start = ((), (), s32[]{:S(2)}) async-start(), calls=%async_computation.8 | async-start | bytes 5591040 | tf_op jit(solution)/shard_map/all_gather | solution.py:742
  102.8 4.5 %copy-start.2 = (f32[2,384,64]{2,1,0:T(8,128)S(1)}, f32[2,384,64]{2,1,0:T(8,128)}, u32[]{:S(2)}) copy-start(f32[2,384,64]{2,1,0:T(8,128)} %copy-done.1) | copy-start | bytes 589828
  103.0 10.3 %collective-permute-start.6 = (bf16[4,48,896]{2,1,0:T(8,128)(2,1)S(1)}, bf16[4,48,896]{2,1,0:T(8,128)(2,1)S(1)}, u32[]{:S(2)}, u32[]{:S(2)}) collective-permute-start(bf16[4,48,896]{2,1,0:T(8,128)(2,1)S(1)} %get-tuple-element.142), channel_id=1, source_target_pairs={{0,12},{2,50},{4,0},{6,54},{8,4},{10,58},{12,8},{14,62},{16,28},{1... | collective-permute-start | bytes 1032200 | tf_op jit(solution)/shard_map/ppermute | solution.py:74
  105.4 7.9 %collective-permute-start.5 = (bf16[4,48,896]{2,1,0:T(8,128)(2,1)S(1)}, bf16[4,48,896]{2,1,0:T(8,128)(2,1)S(1)}, u32[]{:S(2)}, u32[]{:S(2)}) collective-permute-start(bf16[4,48,896]{2,1,0:T(8,128)(2,1)S(1)} %get-tuple-element.143), channel_id=1, source_target_pairs={{0,8},{2,34},{4,12},{6,38},{8,0},{10,42},{12,4},{14,46},{16,24},{1... | collective-permute-start | bytes 1032200 | tf_op jit(solution)/shard_map/ppermute | solution.py:74
  107.4 9.6 %collective-permute-start.4 = (bf16[4,48,896]{2,1,0:T(8,128)(2,1)S(1)}, bf16[4,48,896]{2,1,0:T(8,128)(2,1)S(1)}, u32[]{:S(2)}, u32[]{:S(2)}) collective-permute-start(bf16[4,48,896]{2,1,0:T(8,128)(2,1)S(1)} %get-tuple-element.144), channel_id=1, source_target_pairs={{0,4},{2,18},{4,8},{6,22},{8,12},{10,26},{12,0},{14,30},{16,20},{1... | collective-permute-start | bytes 1032200 | tf_op jit(solution)/shard_map/ppermute | solution.py:74
  117.2 4.6 %collective-permute-start.7 = (bf16[48,896]{1,0:T(8,128)(2,1)S(1)}, bf16[48,896]{1,0:T(8,128)(2,1)S(1)}, u32[]{:S(2)}, u32[]{:S(2)}) collective-permute-start(bf16[48,896]{1,0:T(8,128)(2,1)S(1)} %get-tuple-element.148), channel_id=1, source_target_pairs={{0,1},{1,64},{64,65},{65,0},{2,3},{3,66},{66,67},{67,2},{4,5},{5,6... | collective-permute-start | bytes 258056 | tf_op jit(solution)/shard_map/ppermute | solution.py:74
  117.6 4.3 %collective-permute-start.9 = (bf16[48,896]{1,0:T(8,128)(2,1)S(1)}, bf16[48,896]{1,0:T(8,128)(2,1)S(1)}, u32[]{:S(2)}, u32[]{:S(2)}) collective-permute-start(bf16[48,896]{1,0:T(8,128)(2,1)S(1)} %get-tuple-element.149), channel_id=1, source_target_pairs={{0,65},{1,0},{64,1},{65,64},{2,67},{3,2},{66,3},{67,66},{4,69},{5,... | collective-permute-start | bytes 258056 | tf_op jit(solution)/shard_map/ppermute | solution.py:74
  120.0 4.8 %collective-permute-start.8 = (bf16[48,896]{1,0:T(8,128)(2,1)S(1)}, bf16[48,896]{1,0:T(8,128)(2,1)S(1)}, u32[]{:S(2)}, u32[]{:S(2)}) collective-permute-start(bf16[48,896]{1,0:T(8,128)(2,1)S(1)} %get-tuple-element.150), channel_id=1, source_target_pairs={{0,64},{1,65},{64,0},{65,1},{2,66},{3,67},{66,2},{67,3},{4,68},{5,... | collective-permute-start | bytes 258056 | tf_op jit(solution)/shard_map/ppermute | solution.py:74
  142.9 6.8 %copy-start.9 = (bf16[48,3072]{1,0:T(8,128)(2,1)S(1)}, bf16[48,3072]{1,0:T(8,128)(2,1)}, u32[]{:S(2)}) copy-start(bf16[48,3072]{1,0:T(8,128)(2,1)} %get-tuple-element.99) | copy-start | bytes 884740
  142.9 6.8 %copy-start.10 = (f32[48,768]{1,0:T(8,128)S(1)}, f32[48,768]{1,0:T(8,128)}, u32[]{:S(2)}) copy-start(f32[48,768]{1,0:T(8,128)} %get-tuple-element.98) | copy-start | bytes 442372
  145.8 12.9 %all-to-all-start.4 = ((bf16[32,24,256]{2,1,0:T(8,128)(2,1)}), bf16[32,24,256]{2,1,0:T(8,128)(2,1)S(1)}, u32[]{:S(2)}, u32[]{:S(2)}) async-start(bf16[32,24,256]{2,1,0:T(8,128)(2,1)} %pad_maximum_fusion.1), calls=%async_computation.4 | async-start | bytes 786432 | tf_op jit(solution)/shard_map/all_to_all | solution.py:39
  149.7 3.3 %copy-start.3 = (bf16[1,256,768]{2,1,0:T(8,128)(2,1)S(1)}, bf16[1,256,768]{2,1,0:T(8,128)(2,1)}, u32[]{:S(2)}) copy-start(bf16[1,256,768]{2,1,0:T(8,128)(2,1)} %param.16) | copy-start | bytes 1179652
  189.8 9.4 %collective-permute-start.10 = (bf16[64,24,640]{2,1,0:T(8,128)(2,1)S(1)}, bf16[64,24,640]{2,1,0:T(8,128)(2,1)}, u32[]{:S(2)}, u32[]{:S(2)}) collective-permute-start(bf16[64,24,640]{2,1,0:T(8,128)(2,1)S(1)} %all_to_all.36.own_ref), channel_id=1, source_target_pairs={{0,2},{2,0},{1,3},{3,1},{4,6},{6,4},{5,7},{7,5},{8,10},{10,8},{9,1... | collective-permute-start | bytes 5898248 | tf_op jit(solution)/shard_map/ppermute | solution.py:773
  195.7 17.8 %all-to-all-start.6 = ((bf16[16,48,256]{2,1,0:T(8,128)(2,1)}), bf16[16,48,256]{2,1,0:T(8,128)(2,1)S(1)}, u32[]{:S(2)}, u32[]{:S(2)}) async-start(bf16[16,48,256]{2,1,0:T(8,128)(2,1)} %bitcast.39), calls=%async_computation.6 | async-start | bytes 786432 | tf_op jit(solution)/shard_map/all_to_all | solution.py:39
  199.2 6.2 %copy-start.11 = (f32[768]{0:T(1024)S(1)}, f32[768]{0:T(1024)}, u32[]{:S(2)}) copy-start(f32[768]{0:T(1024)} %gain_ref.3) | copy-start | bytes 9220
  199.2 6.2 %copy-start.12 = (f32[768]{0:T(1024)S(1)}, f32[768]{0:T(1024)}, u32[]{:S(2)}) copy-start(f32[768]{0:T(1024)} %bias_ref.1) | copy-start | bytes 9220
  205.3 17.8 %copy-start.13 = (f32[768]{0:T(1024)}, f32[768]{0:T(1024)S(1)}, u32[]{:S(2)}) copy-start(f32[768]{0:T(1024)S(1)} %get-tuple-element.129) | copy-start | bytes 9220
  213.5 0.7 copy-start.5
  214.3 15.0 %collective-permute-start.11 = (bf16[64,48,896]{2,1,0:T(8,128)(2,1)}, bf16[64,48,896]{2,1,0:T(8,128)(2,1)S(1)}, u32[]{:S(2)}, u32[]{:S(2)}) collective-permute-start(bf16[64,48,896]{2,1,0:T(8,128)(2,1)} %bitcast.80), channel_id=1, source_target_pairs={{0,2},{2,0},{1,3},{3,1},{4,6},{6,4},{5,7},{7,5},{8,10},{10,8},{9,1... | collective-permute-start | bytes 16515080 | tf_op jit(solution)/shard_map/ppermute | solution.py:79
  215.3 2.6 %copy-start = (bf16[3072,896]{1,0:T(8,128)(2,1)S(1)}, bf16[3072,896]{1,0:T(8,128)(2,1)}, u32[]{:S(2)}) copy-start(bf16[3072,896]{1,0:T(8,128)(2,1)} %all-gather.6.cloned.1.call-done) | copy-start | bytes 16515076
Sparse Core Ops, SparseCore 0:
  29.1 48.5 all-gather.3
  125.6 87.7 all-gather.5
